TPU v7x, 32 devices: a whole 2x2x4 slice. The times are simulated.
32 devices in a mesh: blk: 8 (over y, x, core), col: 4 (over z).
Axes of the slice: x: 2, y: 2, z: 4, core: 2. Of those that a mesh axis runs over, the one named last changes fastest.
Arguments:
- three_index: float32 [4096, 12, 4096], P('blk', None, 'col'), may hold values from -6 to 6
- coefficients: float32 [4096, 1024], P('col', 'blk'), may hold values from -0.0078125 to 0.0078125
Outputs:
- exchange_matrix: float32 [4096, 4096], P(('blk', 'col'))
All inputs are finite; a program needn't handle non-finite values.
Results may differ from a plain program's by a relative error of at most 0.000065.
Values sent between devices are 32-bit elements; how exact they have to be, the bound alone decides.
A program may use at most 128 MiB of HBM per device.

v0:
```python
import jax
import jax.numpy as jnp
from jax import lax
from jax.sharding import PartitionSpec as P


def passed_along(block, axis, distance):
    devices = range(lax.axis_size(axis))
    route = [((i - distance) % len(devices), i) for i in devices]
    return lax.ppermute(block, axis, route)


def gram_tile(own_block, other_block):
    return lax.dot_general(
        own_block,
        other_block,
        (((1,), (1,)), ((), ())),
        precision=lax.Precision.HIGHEST,
        preferred_element_type=jnp.float32,
    )


def on_device(three_index, coefficients):
    row_count = three_index.shape[0]
    aux_count = three_index.shape[1]
    flattened = three_index.reshape(row_count * aux_count, three_index.shape[2])
    partial_x = jnp.dot(
        flattened,
        lax.all_gather(coefficients, "blk", axis=1, tiled=True),
        precision=lax.Precision.HIGHEST,
        preferred_element_type=jnp.float32,
    )
    partial_x = partial_x.reshape(row_count, aux_count, partial_x.shape[1])
    half_x = lax.psum_scatter(partial_x, "col", scatter_dimension=2, tiled=True)
    own_block = half_x.reshape(row_count, aux_count * half_x.shape[2])
    cycle_length = lax.axis_size("blk")
    cycle_place = lax.axis_index("blk")

    def place_tile(exchange_part, block_tile, block_index):
        column = jnp.mod(block_index, cycle_length) * row_count
        return lax.dynamic_update_slice(exchange_part, block_tile, (jnp.int32(0), column))

    exchange_part = jnp.zeros((row_count, row_count * cycle_length), jnp.float32)
    exchange_part = place_tile(exchange_part, gram_tile(own_block, own_block), cycle_place)

    def advance(step_index, carry):
        moving, exchange_part = carry
        moving = passed_along(moving, "blk", 1)
        exchange_part = place_tile(
            exchange_part, gram_tile(own_block, moving), cycle_place - step_index
        )
        return (moving, exchange_part)

    moving, exchange_part = lax.fori_loop(1, cycle_length, advance, (own_block, exchange_part))
    return lax.psum_scatter(exchange_part, "col", scatter_dimension=0, tiled=True)


def solution(mesh):
    return jax.shard_map(
        on_device,
        mesh=mesh,
        in_specs=(P("blk", None, "col"), P("col", "blk")),
        out_specs=P(("blk", "col"), None),
        check_vma=False,
    )
```

profile of v0, /device:TPU:0, one launch (start us, length us, event | category | flops | bytes accessed | tf_op | source)
XLA Modules:
  0.0 1378.1 jit_solution(3517121874826497322)
XLA Ops:
  6.5 0.7 all-gather.2.cloned.1.call-update
  7.3 0.0 reduce-scatter.3.cloned.1.call-start
  7.3 42.1 %all-gather.2.cloned.1.call-done = f32[1024,1024]{1,0:T(8,128)} async-done(((f32[1024,128]{1,0:T(8,128)}), f32[1024,1024]{1,0:T(8,128)}) %all-gather.2.cloned.1.call-update) | async-done | bytes 4194320 | tf_op jit(solution)/shard_map/all_gather | solution.py:29
  49.4 88.9 %fusion = f32[512,12,1024]{2,0,1:T(8,128)} fusion(f32[512,12,1024]{2,0,1:T(8,128)} %param.4, f32[1024,1024]{1,0:T(8,128)} %all-gather.2.cloned.1.call-done), kind=kOutput, calls=%fused_computation.1 | convolution fusion | flops 77309411328 | bytes 54525952 | tf_op jit(solution)/shard_map/dot_general | solution.py:27
  138.3 0.0 reduce-scatter.3.cloned.1.call-update
  138.4 0.2 reduce-scatter.5.cloned.1.call-start
  138.6 414.3 %reduce-scatter.3.cloned.1.call-done = f32[512,12,256]{2,0,1:T(8,128)} async-done(((f32[512,12,1024]{2,0,1:T(8,128)}), f32[512,12,256]{2,0,1:T(8,128)}) %reduce-scatter.3.cloned.1.call-update) | async-done | bytes 6291472 | tf_op jit(solution)/shard_map/reduce_scatter | solution.py:34
  552.9 6.6 copy.3
  559.5 6.8 copy.4
  566.3 6.4 copy.9
  572.7 1.0 broadcast_in_dim.3
  573.7 10.5 fusion.2
  584.2 0.0 copy-start
  584.2 3.2 copy-done
  587.5 638.6 %while.17 = (s32[]{:T(128)}, f32[512,3072]{1,0:T(8,128)}, f32[512,4096]{1,0:T(8,128)}, f32[512,3072]{1,0:T(8,128)}, s32[]{:T(128)}, /*index=5*/s32[]{:T(128)}, s...) while((s32[]{:T(128)}, f32[512,3072]{1,0:T(8,128)}, f32[512,4096]{1,0:T(8,128)}, ...), condition=%wide.region_2.3_spmd, body=%wide.region_1.2_spmd.sunk | while | flops 9663676416 | bytes 70254952 | solution.py:54
  587.5 0.0 collective-permute-start
  587.5 71.6 %collective-permute-done = f32[512,3072]{1,0:T(8,128)} collective-permute-done((f32[512,3072]{1,0:T(8,128)}, f32[512,3072]{1,0:T(8,128)}, u32[]{:S(2)}, u32[]{:S(2)}) %collective-permute-start) | collective-permute-done | bytes 6291488 | tf_op jit(solution)/shard_map/while/body/eval_jaxpr/ppermute | solution.py:10
  659.1 6.3 copy.15
  665.3 0.0 slice-done
  665.3 13.4 convolution_dynamic-update-slice_fusion.2
  678.7 0.0 collective-permute-start
  678.7 71.6 %collective-permute-done = f32[512,3072]{1,0:T(8,128)} collective-permute-done((f32[512,3072]{1,0:T(8,128)}, f32[512,3072]{1,0:T(8,128)}, u32[]{:S(2)}, u32[]{:S(2)}) %collective-permute-start) | collective-permute-done | bytes 6291488 | tf_op jit(solution)/shard_map/while/body/eval_jaxpr/ppermute | solution.py:10
  750.3 6.3 copy.15
  756.6 13.3 convolution_dynamic-update-slice_fusion.2
  769.9 0.0 collective-permute-start
  769.9 71.6 %collective-permute-done = f32[512,3072]{1,0:T(8,128)} collective-permute-done((f32[512,3072]{1,0:T(8,128)}, f32[512,3072]{1,0:T(8,128)}, u32[]{:S(2)}, u32[]{:S(2)}) %collective-permute-start) | collective-permute-done | bytes 6291488 | tf_op jit(solution)/shard_map/while/body/eval_jaxpr/ppermute | solution.py:10
  841.5 6.3 copy.15
  847.8 0.0 slice-done
  847.8 13.4 convolution_dynamic-update-slice_fusion.2
  861.1 0.0 collective-permute-start
  861.1 71.6 %collective-permute-done = f32[512,3072]{1,0:T(8,128)} collective-permute-done((f32[512,3072]{1,0:T(8,128)}, f32[512,3072]{1,0:T(8,128)}, u32[]{:S(2)}, u32[]{:S(2)}) %collective-permute-start) | collective-permute-done | bytes 6291488 | tf_op jit(solution)/shard_map/while/body/eval_jaxpr/ppermute | solution.py:10
  932.7 6.3 copy.15
  939.0 0.0 slice-done.1
  939.0 13.3 convolution_dynamic-update-slice_fusion.2
  952.3 0.0 collective-permute-start
  952.3 71.6 %collective-permute-done = f32[512,3072]{1,0:T(8,128)} collective-permute-done((f32[512,3072]{1,0:T(8,128)}, f32[512,3072]{1,0:T(8,128)}, u32[]{:S(2)}, u32[]{:S(2)}) %collective-permute-start) | collective-permute-done | bytes 6291488 | tf_op jit(solution)/shard_map/while/body/eval_jaxpr/ppermute | solution.py:10
  1023.9 6.3 copy.15
  1030.2 13.3 convolution_dynamic-update-slice_fusion.2
  1043.5 0.0 collective-permute-start
  1043.5 71.6 %collective-permute-done = f32[512,3072]{1,0:T(8,128)} collective-permute-done((f32[512,3072]{1,0:T(8,128)}, f32[512,3072]{1,0:T(8,128)}, u32[]{:S(2)}, u32[]{:S(2)}) %collective-permute-start) | collective-permute-done | bytes 6291488 | tf_op jit(solution)/shard_map/while/body/eval_jaxpr/ppermute | solution.py:10
  1115.1 6.3 copy.15
  1121.4 13.4 convolution_dynamic-update-slice_fusion.2
  1134.8 0.0 collective-permute-start
  1134.8 71.6 %collective-permute-done = f32[512,3072]{1,0:T(8,128)} collective-permute-done((f32[512,3072]{1,0:T(8,128)}, f32[512,3072]{1,0:T(8,128)}, u32[]{:S(2)}, u32[]{:S(2)}) %collective-permute-start) | collective-permute-done | bytes 6291488 | tf_op jit(solution)/shard_map/while/body/eval_jaxpr/ppermute | solution.py:10
  1206.4 6.3 copy.15
  1212.7 13.4 convolution_dynamic-update-slice_fusion.2
  1226.0 0.0 reduce-scatter.5.cloned.1.call-update
  1226.1 145.5 %reduce-scatter.5.cloned.1.call-done = f32[128,4096]{1,0:T(8,128)} async-done(((f32[512,4096]{1,0:T(8,128)}), f32[128,4096]{1,0:T(8,128)}) %reduce-scatter.5.cloned.1.call-update) | async-done | bytes 2097168 | tf_op jit(solution)/shard_map/reduce_scatter | solution.py:55
  (38 shorter events, 0.1 us)
Async XLA Ops:
  6.5 42.9 %all-gather.2.cloned.1.call-start = ((), (), s32[]{:S(2)}) async-start(), calls=%async_computation.2 | async-start | bytes 4718592 | tf_op jit(solution)/shard_map/all_gather | solution.py:29
  7.3 545.7 %reduce-scatter.3.cloned.1.call-start = ((), (), s32[]{:S(2)}) async-start(), calls=%async_computation.3 | async-start | bytes 31457280 | tf_op jit(solution)/shard_map/reduce_scatter | solution.py:34
  138.4 1233.2 %reduce-scatter.5.cloned.1.call-start = ((), (), s32[]{:S(2)}) async-start(), calls=%async_computation.4 | async-start | bytes 10485760 | tf_op jit(solution)/shard_map/reduce_scatter | solution.py:55
  559.5 14.2 %slice-start.2 = ((s8[6291456]{0:T(1024)(128)(4,1)}), s8[2097152]{0:T(1024)(128)(4,1)S(1)}, s32[]{:S(2)}) async-start(s8[6291456]{0:T(1024)(128)(4,1)} %bitcast.19), calls=%async_computation.7 | async-start | bytes 4194304
  566.3 7.4 slice-start.3
  584.2 3.2 copy-start
  587.5 71.6 %collective-permute-start = (f32[512,3072]{1,0:T(8,128)}, f32[512,3072]{1,0:T(8,128)}, u32[]{:S(2)}, u32[]{:S(2)}) collective-permute-start(f32[512,3072]{1,0:T(8,128)} %get-tuple-element.197), channel_id=1, source_target_pairs={{28,0},{0,4},{4,8},{8,12},{12,16},{16,20},{20,24},{24,28},{29,1},{... | collective-permute-start | bytes 18874376 | tf_op jit(solution)/shard_map/while/body/eval_jaxpr/ppermute | solution.py:10
  587.5 77.9 %slice-start = ((s8[6291456]{0:T(1024)(128)(4,1)}), s8[2097152]{0:T(1024)(128)(4,1)S(1)}, s32[]{:S(2)}) async-start(s8[6291456]{0:T(1024)(128)(4,1)} %bitcast.17), calls=%async_computation.5 | async-start | bytes 4194304 | tf_op jit(solution)/shard_map/while
  587.5 77.9 %slice-start.1 = ((s8[6291456]{0:T(1024)(128)(4,1)}), s8[4194304]{0:T(1024)(128)(4,1)S(1)}, s32[]{:S(2)}) async-start(s8[6291456]{0:T(1024)(128)(4,1)} %bitcast.17), calls=%async_computation.6 | async-start | bytes 8388608 | tf_op jit(solution)/shard_map/while
  678.7 71.6 %collective-permute-start = (f32[512,3072]{1,0:T(8,128)}, f32[512,3072]{1,0:T(8,128)}, u32[]{:S(2)}, u32[]{:S(2)}) collective-permute-start(f32[512,3072]{1,0:T(8,128)} %get-tuple-element.197), channel_id=1, source_target_pairs={{28,0},{0,4},{4,8},{8,12},{12,16},{16,20},{20,24},{24,28},{29,1},{... | collective-permute-start | bytes 18874376 | tf_op jit(solution)/shard_map/while/body/eval_jaxpr/ppermute | solution.py:10
  678.7 77.9 %slice-start = ((s8[6291456]{0:T(1024)(128)(4,1)}), s8[2097152]{0:T(1024)(128)(4,1)S(1)}, s32[]{:S(2)}) async-start(s8[6291456]{0:T(1024)(128)(4,1)} %bitcast.17), calls=%async_computation.5 | async-start | bytes 4194304 | tf_op jit(solution)/shard_map/while
  678.7 77.9 %slice-start.1 = ((s8[6291456]{0:T(1024)(128)(4,1)}), s8[4194304]{0:T(1024)(128)(4,1)S(1)}, s32[]{:S(2)}) async-start(s8[6291456]{0:T(1024)(128)(4,1)} %bitcast.17), calls=%async_computation.6 | async-start | bytes 8388608 | tf_op jit(solution)/shard_map/while
  769.9 71.6 %collective-permute-start = (f32[512,3072]{1,0:T(8,128)}, f32[512,3072]{1,0:T(8,128)}, u32[]{:S(2)}, u32[]{:S(2)}) collective-permute-start(f32[512,3072]{1,0:T(8,128)} %get-tuple-element.197), channel_id=1, source_target_pairs={{28,0},{0,4},{4,8},{8,12},{12,16},{16,20},{20,24},{24,28},{29,1},{... | collective-permute-start | bytes 18874376 | tf_op jit(solution)/shard_map/while/body/eval_jaxpr/ppermute | solution.py:10
  769.9 77.9 %slice-start = ((s8[6291456]{0:T(1024)(128)(4,1)}), s8[2097152]{0:T(1024)(128)(4,1)S(1)}, s32[]{:S(2)}) async-start(s8[6291456]{0:T(1024)(128)(4,1)} %bitcast.17), calls=%async_computation.5 | async-start | bytes 4194304 | tf_op jit(solution)/shard_map/while
  769.9 77.9 %slice-start.1 = ((s8[6291456]{0:T(1024)(128)(4,1)}), s8[4194304]{0:T(1024)(128)(4,1)S(1)}, s32[]{:S(2)}) async-start(s8[6291456]{0:T(1024)(128)(4,1)} %bitcast.17), calls=%async_computation.6 | async-start | bytes 8388608 | tf_op jit(solution)/shard_map/while
  861.1 71.6 %collective-permute-start = (f32[512,3072]{1,0:T(8,128)}, f32[512,3072]{1,0:T(8,128)}, u32[]{:S(2)}, u32[]{:S(2)}) collective-permute-start(f32[512,3072]{1,0:T(8,128)} %get-tuple-element.197), channel_id=1, source_target_pairs={{28,0},{0,4},{4,8},{8,12},{12,16},{16,20},{20,24},{24,28},{29,1},{... | collective-permute-start | bytes 18874376 | tf_op jit(solution)/shard_map/while/body/eval_jaxpr/ppermute | solution.py:10
  861.1 77.9 %slice-start = ((s8[6291456]{0:T(1024)(128)(4,1)}), s8[2097152]{0:T(1024)(128)(4,1)S(1)}, s32[]{:S(2)}) async-start(s8[6291456]{0:T(1024)(128)(4,1)} %bitcast.17), calls=%async_computation.5 | async-start | bytes 4194304 | tf_op jit(solution)/shard_map/while
  861.1 77.9 %slice-start.1 = ((s8[6291456]{0:T(1024)(128)(4,1)}), s8[4194304]{0:T(1024)(128)(4,1)S(1)}, s32[]{:S(2)}) async-start(s8[6291456]{0:T(1024)(128)(4,1)} %bitcast.17), calls=%async_computation.6 | async-start | bytes 8388608 | tf_op jit(solution)/shard_map/while
  952.3 71.6 %collective-permute-start = (f32[512,3072]{1,0:T(8,128)}, f32[512,3072]{1,0:T(8,128)}, u32[]{:S(2)}, u32[]{:S(2)}) collective-permute-start(f32[512,3072]{1,0:T(8,128)} %get-tuple-element.197), channel_id=1, source_target_pairs={{28,0},{0,4},{4,8},{8,12},{12,16},{16,20},{20,24},{24,28},{29,1},{... | collective-permute-start | bytes 18874376 | tf_op jit(solution)/shard_map/while/body/eval_jaxpr/ppermute | solution.py:10
  952.3 77.9 %slice-start = ((s8[6291456]{0:T(1024)(128)(4,1)}), s8[2097152]{0:T(1024)(128)(4,1)S(1)}, s32[]{:S(2)}) async-start(s8[6291456]{0:T(1024)(128)(4,1)} %bitcast.17), calls=%async_computation.5 | async-start | bytes 4194304 | tf_op jit(solution)/shard_map/while
  952.3 77.9 %slice-start.1 = ((s8[6291456]{0:T(1024)(128)(4,1)}), s8[4194304]{0:T(1024)(128)(4,1)S(1)}, s32[]{:S(2)}) async-start(s8[6291456]{0:T(1024)(128)(4,1)} %bitcast.17), calls=%async_computation.6 | async-start | bytes 8388608 | tf_op jit(solution)/shard_map/while
  1043.5 71.6 %collective-permute-start = (f32[512,3072]{1,0:T(8,128)}, f32[512,3072]{1,0:T(8,128)}, u32[]{:S(2)}, u32[]{:S(2)}) collective-permute-start(f32[512,3072]{1,0:T(8,128)} %get-tuple-element.197), channel_id=1, source_target_pairs={{28,0},{0,4},{4,8},{8,12},{12,16},{16,20},{20,24},{24,28},{29,1},{... | collective-permute-start | bytes 18874376 | tf_op jit(solution)/shard_map/while/body/eval_jaxpr/ppermute | solution.py:10
  1043.5 77.9 %slice-start = ((s8[6291456]{0:T(1024)(128)(4,1)}), s8[2097152]{0:T(1024)(128)(4,1)S(1)}, s32[]{:S(2)}) async-start(s8[6291456]{0:T(1024)(128)(4,1)} %bitcast.17), calls=%async_computation.5 | async-start | bytes 4194304 | tf_op jit(solution)/shard_map/while
  1043.5 77.9 %slice-start.1 = ((s8[6291456]{0:T(1024)(128)(4,1)}), s8[4194304]{0:T(1024)(128)(4,1)S(1)}, s32[]{:S(2)}) async-start(s8[6291456]{0:T(1024)(128)(4,1)} %bitcast.17), calls=%async_computation.6 | async-start | bytes 8388608 | tf_op jit(solution)/shard_map/while
  1134.8 71.6 %collective-permute-start = (f32[512,3072]{1,0:T(8,128)}, f32[512,3072]{1,0:T(8,128)}, u32[]{:S(2)}, u32[]{:S(2)}) collective-permute-start(f32[512,3072]{1,0:T(8,128)} %get-tuple-element.197), channel_id=1, source_target_pairs={{28,0},{0,4},{4,8},{8,12},{12,16},{16,20},{20,24},{24,28},{29,1},{... | collective-permute-start | bytes 18874376 | tf_op jit(solution)/shard_map/while/body/eval_jaxpr/ppermute | solution.py:10
  1134.8 77.9 %slice-start = ((s8[6291456]{0:T(1024)(128)(4,1)}), s8[2097152]{0:T(1024)(128)(4,1)S(1)}, s32[]{:S(2)}) async-start(s8[6291456]{0:T(1024)(128)(4,1)} %bitcast.17), calls=%async_computation.5 | async-start | bytes 4194304 | tf_op jit(solution)/shard_map/while
  1134.8 77.9 %slice-start.1 = ((s8[6291456]{0:T(1024)(128)(4,1)}), s8[4194304]{0:T(1024)(128)(4,1)S(1)}, s32[]{:S(2)}) async-start(s8[6291456]{0:T(1024)(128)(4,1)} %bitcast.17), calls=%async_computation.6 | async-start | bytes 8388608 | tf_op jit(solution)/shard_map/while
Sparse Core Ops, SparseCore 0:
  9.2 40.1 all-gather.1
  138.5 414.3 reduce-scatter.2
  1226.2 145.3 reduce-scatter.4
where the time goes:
time: 1380 us
  waiting for transfers between devices  1100 us (80%)
  matrix products  193 us (14%)
  local copies, waits for them, and re-layouts  67.8 us (5%)
    ppermute x7, waiting for transfers between devices, passed_along(): return lax.ppermute(block, axis, route)  501 us
    reduce_scatter x1, waiting for transfers between devices, on_device(): half_x = lax.psum_scatter(partial_x, 'col', scatter_dimension=2, tiled=True)  414 us
    reduce_scatter x1, waiting for transfers between devices, on_device(): lax.psum_scatter(exchange_part, 'col', scatter_dimension=0, tiled=True)  145 us
    dot_general x8, matrix products, gram_tile(): lax.dot_general(own_block, other_block, (((1,), (1,)), ((), ())), precisi...  104 us
    dot_general x1, matrix products, on_device(): jnp.dot(flattened, lax.all_gather(coefficients, 'blk', axis=1, tiled=True...  88.9 us
    while x35, local copies, waits for them, and re-layouts  43.8 us
    all_gather x1, waiting for transfers between devices, on_device(): lax.all_gather(coefficients, 'blk', axis=1, tiled=True)  42.1 us
  transfers between devices with their start and end apart: 10, of which 10 were waited for; matrix products, arithmetic and copies ran while one was open for 0% of the time, Pallas kernels for 0%

commit v1 on v0

v1 whole, which is shorter than its diff:
```python
import jax
import jax.numpy as jnp
from jax import lax
from jax.sharding import PartitionSpec as P

GROUPS = 6


def exchanged(block, axis, flip):
    route = [(i, i ^ flip) for i in range(lax.axis_size(axis))]
    return lax.ppermute(block, axis, route)


def product(left, right, dims):
    return lax.dot_general(
        left,
        right,
        (dims, ((), ())),
        precision=lax.Precision.HIGH,
        preferred_element_type=jnp.float32,
    )


def blocks_of_others(own, axis):
    count = lax.axis_size(axis)
    held = {0: own}
    far = [j for j in range(2, count, 2)]
    for j in far:
        if count == 8 and j == 6:
            half = own.shape[0] // 2
            first = exchanged(held[2][:half], axis, 4)
            second = exchanged(held[4][half:], axis, 2)
            held[6] = jnp.concatenate([first, second], axis=0)
        else:
            held[j] = exchanged(own, axis, j)
    for j in [0] + far:
        held[j + 1] = exchanged(held[j], axis, 1)
    return [held[j] for j in range(count)]


def on_device(three_index, coefficients):
    row_count, aux_count, _ = three_index.shape
    blk_size = lax.axis_size("blk")
    place = lax.axis_index("blk")
    orbitals = lax.all_gather(coefficients, "blk", axis=1, tiled=True)
    per_group = aux_count // GROUPS
    tiles = None
    for group in range(GROUPS):
        part = three_index[:, group * per_group : (group + 1) * per_group]
        partial_x = jnp.concatenate(
            [product(part[:, p], orbitals, ((1,), (0,))) for p in range(per_group)], axis=0
        )
        half_x = lax.psum_scatter(partial_x, "col", scatter_dimension=1, tiled=True)
        own = jnp.concatenate(
            [half_x[p * row_count : (p + 1) * row_count] for p in range(per_group)], axis=1
        )
        blocks = blocks_of_others(own, "blk")
        terms = [product(own, block, ((1,), (1,))) for block in blocks]
        tiles = terms if tiles is None else [t + u for t, u in zip(tiles, terms)]
    exchange_part = jnp.concatenate(tiles, axis=1)
    rows = lax.psum_scatter(exchange_part, "col", scatter_dimension=0, tiled=True)
    shares = jnp.split(rows, blk_size, axis=1)
    flip = 1
    while flip < blk_size:
        swap = (place & flip) != 0
        shares = [jnp.where(swap, shares[j ^ flip], shares[j]) for j in range(blk_size)]
        flip *= 2
    return jnp.concatenate(shares, axis=1)


def solution(mesh):
    return jax.shard_map(
        on_device,
        mesh=mesh,
        in_specs=(P("blk", None, "col"), P("col", "blk")),
        out_specs=P(("blk", "col"), None),
        check_vma=False,
    )
```

time: 1380 us -> 1010 us (0.73)
  waiting for transfers between devices: 1100 us -> 771 us
  matrix products: 193 us -> 139 us
  local copies, waits for them, and re-layouts: 67.8 us -> 14.1 us
  starting transfers between devices: 0.28 us -> 34.1 us
  other arithmetic: 0.01 us -> 30.3 us
    ppermute x7 -> x48, waiting for transfers between devices: 501 us -> 202 us  [exchanged(): return lax.ppermute(block, axis, route)]
    dot_general x9 -> x60, matrix products: 193 us -> 139 us  [product(): lax.dot_general(left, right, (dims, ((), ())), precision=lax.Precision.HI...]
    while x36 -> x0, local copies, waits for them, and re-layouts: 50.6 us -> none
    ppermute x7 -> x48, starting transfers between devices: 0.02 us -> 33 us  [exchanged(): return lax.ppermute(block, axis, route)]
    reduce_scatter x1 -> x6, waiting for transfers between devices: 414 us -> 382 us  [on_device(): half_x = lax.psum_scatter(partial_x, 'col', scatter_dimension=1, tiled=True)]
    concatenate x0 -> x13, other arithmetic: none -> 23.2 us  [the longest x6 16.5 us: on_device(): jnp.concatenate([product(part[:, p], orbitals, ((1,), (0,))) for p in ran...]
  transfers between devices with their start and end apart: 10 -> 56, of which waited for: 10 -> 24; matrix products, arithmetic and copies ran while one was open for 0% -> 15% of each run, Pallas kernels for 0% -> 0%
where the time goes in v1:
time: 1010 us; the launch traced here: 1000 us
  waiting for transfers between devices  771 us (76%)
  matrix products  139 us (14%)
  starting transfers between devices  34.1 us (3%)
  other arithmetic  30.3 us (3%)
  between operations  15 us (1%)
  local copies, waits for them, and re-layouts  14.1 us (1%)
    reduce_scatter x6, waiting for transfers between devices, on_device(): half_x = lax.psum_scatter(partial_x, 'col', scatter_dimension=1, tiled=True)  382 us
    ppermute x48, waiting for transfers between devices, exchanged(): return lax.ppermute(block, axis, route)  202 us
    reduce_scatter x1, waiting for transfers between devices, on_device(): lax.psum_scatter(exchange_part, 'col', scatter_dimension=0, tiled=True)  144 us
    dot_general x60, matrix products, product(): lax.dot_general(left, right, (dims, ((), ())), precision=lax.Precision.HI...  139 us
    all_gather x1, waiting for transfers between devices, on_device(): orbitals = lax.all_gather(coefficients, 'blk', axis=1, tiled=True)  42.1 us
    ppermute x48, starting transfers between devices, exchanged(): return lax.ppermute(block, axis, route)  33 us
  transfers between devices with their start and end apart: 56, of which 24 were waited for; matrix products, arithmetic and copies ran while one was open for 15% of the time, Pallas kernels for 0%

profile of v1, /device:TPU:0, one launch (start us, length us, event | category | flops | bytes accessed | tf_op | source)
XLA Modules:
  0.0 1003.1 jit_solution(6330246116938891622)
XLA Ops:
  7.3 42.1 %all-gather.2.cloned.1.call-done = f32[1024,1024]{1,0:T(8,128)} async-done(((f32[1024,128]{1,0:T(8,128)}), f32[1024,1024]{1,0:T(8,128)}) %all-gather.2.cloned.1.call-update) | async-done | bytes 4194320 | tf_op jit(solution)/shard_map/all_gather | solution.py:45
  49.4 6.4 fusion.16
  55.9 5.4 fusion.18
  61.2 2.8 pad_maximum_fusion.1
  64.1 6.5 fusion
  70.6 5.5 fusion.2
  76.1 2.8 pad_maximum_fusion.5
  79.4 6.5 fusion.4
  85.9 5.4 fusion.6
  91.2 2.7 pad_maximum_fusion.4
  94.0 6.5 fusion.10
  100.5 5.4 fusion.8
  105.9 2.6 pad_maximum_fusion.3
  108.8 6.5 fusion.20
  115.3 5.4 fusion.22
  120.7 2.8 pad_maximum_fusion
  123.6 6.5 fusion.12
  130.1 5.4 fusion.14
  135.5 2.8 pad_maximum_fusion.2
  138.6 2.4 reduce-scatter.10.cloned.1.call-done
  144.9 75.8 %reduce-scatter.18.cloned.1.call-done = f32[1024,256]{1,0:T(8,128)} async-done(((f32[1024,1024]{1,0:T(8,128)}), f32[1024,256]{1,0:T(8,128)}) %reduce-scatter.18.cloned.1.call-update) | async-done | bytes 1048592 | tf_op jit(solution)/shard_map/reduce_scatter | solution.py:53
  223.1 77.0 %reduce-scatter.16.cloned.1.call-done = f32[1024,256]{1,0:T(8,128)} async-done(((f32[1024,1024]{1,0:T(8,128)}), f32[1024,256]{1,0:T(8,128)}) %reduce-scatter.16.cloned.1.call-update) | async-done | bytes 1048592 | tf_op jit(solution)/shard_map/reduce_scatter | solution.py:53
  303.4 76.3 %reduce-scatter.14.cloned.1.call-done = f32[1024,256]{1,0:T(8,128)} async-done(((f32[1024,1024]{1,0:T(8,128)}), f32[1024,256]{1,0:T(8,128)}) %reduce-scatter.14.cloned.1.call-update) | async-done | bytes 1048592 | tf_op jit(solution)/shard_map/reduce_scatter | solution.py:53
  382.9 76.2 %reduce-scatter.8.cloned.1.call-done = f32[1024,256]{1,0:T(8,128)} async-done(((f32[1024,1024]{1,0:T(8,128)}), f32[1024,256]{1,0:T(8,128)}) %reduce-scatter.8.cloned.1.call-update) | async-done | bytes 1048592 | tf_op jit(solution)/shard_map/reduce_scatter | solution.py:53
  464.5 74.3 %reduce-scatter.12.cloned.1.call-done = f32[1024,256]{1,0:T(8,128)} async-done(((f32[1024,1024]{1,0:T(8,128)}), f32[1024,256]{1,0:T(8,128)}) %reduce-scatter.12.cloned.1.call-update) | async-done | bytes 1048592 | tf_op jit(solution)/shard_map/reduce_scatter | solution.py:53
  556.2 2.7 fusion.92
  564.3 9.9 collective-permute-done.11
  576.7 20.0 %collective-permute-done.10 = f32[512,512]{1,0:T(8,128)S(1)} collective-permute-done((f32[512,512]{1,0:T(8,128)}, f32[512,512]{1,0:T(8,128)S(1)}, u32[]{:S(2)}, u32[]{:S(2)}) %collective-permute-start.10) | collective-permute-done | bytes 1048608 | tf_op jit(solution)/shard_map/ppermute | solution.py:11
  599.2 20.0 %collective-permute-done.9 = f32[512,512]{1,0:T(8,128)S(1)} collective-permute-done((f32[512,512]{1,0:T(8,128)}, f32[512,512]{1,0:T(8,128)S(1)}, u32[]{:S(2)}, u32[]{:S(2)}) %collective-permute-start.9) | collective-permute-done | bytes 1048608 | tf_op jit(solution)/shard_map/ppermute | solution.py:11
  620.2 21.0 %collective-permute-done.8 = f32[512,512]{1,0:T(8,128)S(1)} collective-permute-done((f32[512,512]{1,0:T(8,128)S(1)}, f32[512,512]{1,0:T(8,128)S(1)}, u32[]{:S(2)}, u32[]{:S(2)}) %collective-permute-start.8) | collective-permute-done | bytes 1048608 | tf_op jit(solution)/shard_map/ppermute | solution.py:11
  654.7 11.3 %collective-permute-done.6 = f32[512,512]{1,0:T(8,128)S(1)} collective-permute-done((f32[512,512]{1,0:T(8,128)S(1)}, f32[512,512]{1,0:T(8,128)S(1)}, u32[]{:S(2)}, u32[]{:S(2)}) %collective-permute-start.6) | collective-permute-done | bytes 1048608 | tf_op jit(solution)/shard_map/ppermute | solution.py:11
  667.7 2.3 fusion.51
  672.8 19.8 %collective-permute-done.20 = f32[512,512]{1,0:T(8,128)S(1)} collective-permute-done((f32[512,512]{1,0:T(8,128)S(1)}, f32[512,512]{1,0:T(8,128)S(1)}, u32[]{:S(2)}, u32[]{:S(2)}) %collective-permute-start.20) | collective-permute-done | bytes 1048608 | tf_op jit(solution)/shard_map/ppermute | solution.py:11
  694.1 21.0 %collective-permute-done.18 = f32[512,512]{1,0:T(8,128)S(1)} collective-permute-done((f32[512,512]{1,0:T(8,128)S(1)}, f32[512,512]{1,0:T(8,128)S(1)}, u32[]{:S(2)}, u32[]{:S(2)}) %collective-permute-start.18) | collective-permute-done | bytes 1048608 | tf_op jit(solution)/shard_map/ppermute | solution.py:11
  717.9 8.4 collective-permute-done.32
  727.8 9.7 collective-permute-done.40
  738.2 10.6 %collective-permute-done.38 = f32[256,512]{1,0:T(8,128)S(1)} collective-permute-done((f32[256,512]{1,0:T(8,128)S(1)}, f32[256,512]{1,0:T(8,128)S(1)}, u32[]{:S(2)}, u32[]{:S(2)}) %collective-permute-start.38) | collective-permute-done | bytes 524320 | tf_op jit(solution)/shard_map/ppermute | solution.py:11
  749.4 10.6 %collective-permute-done.36 = f32[256,512]{1,0:T(8,128)S(1)} collective-permute-done((f32[256,512]{1,0:T(8,128)S(1)}, f32[256,512]{1,0:T(8,128)S(1)}, u32[]{:S(2)}, u32[]{:S(2)}) %collective-permute-start.36) | collective-permute-done | bytes 524320 | tf_op jit(solution)/shard_map/ppermute | solution.py:11
  760.6 10.6 %collective-permute-done.34 = f32[256,512]{1,0:T(8,128)S(1)} collective-permute-done((f32[256,512]{1,0:T(8,128)S(1)}, f32[256,512]{1,0:T(8,128)S(1)}, u32[]{:S(2)}, u32[]{:S(2)}) %collective-permute-start.34) | collective-permute-done | bytes 524320 | tf_op jit(solution)/shard_map/ppermute | solution.py:11
  771.9 9.0 collective-permute-done.30
  784.0 11.8 %collective-permute-done.35 = f32[256,512]{1,0:T(8,128)S(1)} collective-permute-done((f32[256,512]{1,0:T(8,128)S(1)}, f32[256,512]{1,0:T(8,128)S(1)}, u32[]{:S(2)}, u32[]{:S(2)}) %collective-permute-start.35) | collective-permute-done | bytes 524320 | tf_op jit(solution)/shard_map/ppermute | solution.py:11
  796.9 7.6 collective-permute-done.31
  823.8 2.3 fusion.59
  830.3 2.3 fusion.67
  838.4 2.4 fusion.71
  840.8 144.3 %reduce-scatter.20.cloned.1.call-done = f32[128,4096]{0,1:T(8,128)} async-done(((f32[512,4096]{0,1:T(8,128)}), f32[128,4096]{0,1:T(8,128)}) %reduce-scatter.20.cloned.1.call-update) | async-done | bytes 2097168 | tf_op jit(solution)/shard_map/reduce_scatter | solution.py:61
  985.1 2.5 select_dynamic-update-slice_fusion.7
  993.0 2.9 copy.3
  (217 shorter events, 113.3 us)
Async XLA Ops:
  6.5 42.9 %all-gather.2.cloned.1.call-start = ((), (), s32[]{:S(2)}) async-start(), calls=%async_computation.7 | async-start | bytes 4718592 | tf_op jit(solution)/shard_map/all_gather | solution.py:45
  7.3 133.7 %reduce-scatter.10.cloned.1.call-start = ((), (), s32[]{:S(2)}) async-start(), calls=%async_computation.9 | async-start | bytes 5242880 | tf_op jit(solution)/shard_map/reduce_scatter | solution.py:53
  64.1 156.6 %reduce-scatter.18.cloned.1.call-start = ((), (), s32[]{:S(2)}) async-start(), calls=%async_computation.13 | async-start | bytes 5242880 | tf_op jit(solution)/shard_map/reduce_scatter | solution.py:53
  78.9 221.2 %reduce-scatter.16.cloned.1.call-start = ((), (), s32[]{:S(2)}) async-start(), calls=%async_computation.12 | async-start | bytes 5242880 | tf_op jit(solution)/shard_map/reduce_scatter | solution.py:53
  94.0 285.7 %reduce-scatter.14.cloned.1.call-start = ((), (), s32[]{:S(2)}) async-start(), calls=%async_computation.11 | async-start | bytes 5242880 | tf_op jit(solution)/shard_map/reduce_scatter | solution.py:53
  108.5 350.6 %reduce-scatter.8.cloned.1.call-start = ((), (), s32[]{:S(2)}) async-start(), calls=%async_computation.8 | async-start | bytes 5242880 | tf_op jit(solution)/shard_map/reduce_scatter | solution.py:53
  123.5 415.3 %reduce-scatter.12.cloned.1.call-start = ((), (), s32[]{:S(2)}) async-start(), calls=%async_computation.10 | async-start | bytes 5242880 | tf_op jit(solution)/shard_map/reduce_scatter | solution.py:53
  138.3 846.8 %reduce-scatter.20.cloned.1.call-start = ((), (), s32[]{:S(2)}) async-start(), calls=%async_computation.14 | async-start | bytes 10485760 | tf_op jit(solution)/shard_map/reduce_scatter | solution.py:61
  143.4 402.3 %collective-permute-start.1 = (f32[512,512]{1,0:T(8,128)}, f32[512,512]{1,0:T(8,128)}, u32[]{:S(2)}, u32[]{:S(2)}) collective-permute-start(f32[512,512]{1,0:T(8,128)} %pad_maximum_fusion.7), channel_id=1, source_target_pairs={{0,4},{4,0},{8,12},{12,8},{16,20},{20,16},{24,28},{28,24},{1,5},{5... | collective-permute-start | bytes 3145736 | tf_op jit(solution)/shard_map/ppermute | solution.py:11
  143.4 417.2 %collective-permute-start.7 = (f32[512,512]{1,0:T(8,128)}, f32[512,512]{1,0:T(8,128)}, u32[]{:S(2)}, u32[]{:S(2)}) collective-permute-start(f32[512,512]{1,0:T(8,128)} %pad_maximum_fusion.7), channel_id=1, source_target_pairs={{0,8},{4,12},{8,0},{12,4},{16,24},{20,28},{24,16},{28,20},{1,9},{5... | collective-permute-start | bytes 3145736 | tf_op jit(solution)/shard_map/ppermute | solution.py:11
  223.1 324.9 %collective-permute-start.5 = (f32[512,512]{1,0:T(8,128)}, f32[512,512]{1,0:T(8,128)}, u32[]{:S(2)}, u32[]{:S(2)}) collective-permute-start(f32[512,512]{1,0:T(8,128)} %pad_maximum_fusion.11), channel_id=1, source_target_pairs={{0,4},{4,0},{8,12},{12,8},{16,20},{20,16},{24,28},{28,24},{1,5},{5... | collective-permute-start | bytes 3145736 | tf_op jit(solution)/shard_map/ppermute | solution.py:11
  303.4 248.4 %collective-permute-start.4 = (f32[512,512]{1,0:T(8,128)}, f32[512,512]{1,0:T(8,128)}, u32[]{:S(2)}, u32[]{:S(2)}) collective-permute-start(f32[512,512]{1,0:T(8,128)} %pad_maximum_fusion.10), channel_id=1, source_target_pairs={{0,4},{4,0},{8,12},{12,8},{16,20},{20,16},{24,28},{28,24},{1,5},{5... | collective-permute-start | bytes 3145736 | tf_op jit(solution)/shard_map/ppermute | solution.py:11
  382.9 171.8 %collective-permute-start.3 = (f32[512,512]{1,0:T(8,128)}, f32[512,512]{1,0:T(8,128)}, u32[]{:S(2)}, u32[]{:S(2)}) collective-permute-start(f32[512,512]{1,0:T(8,128)} %pad_maximum_fusion.9), channel_id=1, source_target_pairs={{0,4},{4,0},{8,12},{12,8},{16,20},{20,16},{24,28},{28,24},{1,5},{5... | collective-permute-start | bytes 3145736 | tf_op jit(solution)/shard_map/ppermute | solution.py:11
  545.7 13.1 %collective-permute-start.2 = (f32[512,512]{1,0:T(8,128)S(1)}, f32[512,512]{1,0:T(8,128)S(1)}, u32[]{:S(2)}, u32[]{:S(2)}) collective-permute-start(f32[512,512]{1,0:T(8,128)S(1)} %pad_maximum_fusion.8), channel_id=1, source_target_pairs={{0,4},{4,0},{8,12},{12,8},{16,20},{20,16},{24,28},{28,24},{1,5},{5... | collective-permute-start | bytes 3145736 | tf_op jit(solution)/shard_map/ppermute | solution.py:11
  548.0 26.2 %collective-permute-start.11 = (f32[512,512]{1,0:T(8,128)}, f32[512,512]{1,0:T(8,128)S(1)}, u32[]{:S(2)}, u32[]{:S(2)}) collective-permute-start(f32[512,512]{1,0:T(8,128)} %pad_maximum_fusion.11), channel_id=1, source_target_pairs={{0,8},{4,12},{8,0},{12,4},{16,24},{20,28},{24,16},{28,20},{1,9},{5... | collective-permute-start | bytes 3145736 | tf_op jit(solution)/shard_map/ppermute | solution.py:11
  551.8 44.9 %collective-permute-start.10 = (f32[512,512]{1,0:T(8,128)}, f32[512,512]{1,0:T(8,128)S(1)}, u32[]{:S(2)}, u32[]{:S(2)}) collective-permute-start(f32[512,512]{1,0:T(8,128)} %pad_maximum_fusion.10), channel_id=1, source_target_pairs={{0,8},{4,12},{8,0},{12,4},{16,24},{20,28},{24,16},{28,20},{1,9},{5... | collective-permute-start | bytes 3145736 | tf_op jit(solution)/shard_map/ppermute | solution.py:11
  554.7 64.5 %collective-permute-start.9 = (f32[512,512]{1,0:T(8,128)}, f32[512,512]{1,0:T(8,128)S(1)}, u32[]{:S(2)}, u32[]{:S(2)}) collective-permute-start(f32[512,512]{1,0:T(8,128)} %pad_maximum_fusion.9), channel_id=1, source_target_pairs={{0,8},{4,12},{8,0},{12,4},{16,24},{20,28},{24,16},{28,20},{1,9},{5... | collective-permute-start | bytes 3145736 | tf_op jit(solution)/shard_map/ppermute | solution.py:11
  558.9 82.4 %collective-permute-start.8 = (f32[512,512]{1,0:T(8,128)S(1)}, f32[512,512]{1,0:T(8,128)S(1)}, u32[]{:S(2)}, u32[]{:S(2)}) collective-permute-start(f32[512,512]{1,0:T(8,128)S(1)} %pad_maximum_fusion.8), channel_id=1, source_target_pairs={{0,8},{4,12},{8,0},{12,4},{16,24},{20,28},{24,16},{28,20},{1,9},{5... | collective-permute-start | bytes 3145736 | tf_op jit(solution)/shard_map/ppermute | solution.py:11
  560.6 83.2 %collective-permute-start.19 = (f32[512,512]{1,0:T(8,128)}, f32[512,512]{1,0:T(8,128)S(1)}, u32[]{:S(2)}, u32[]{:S(2)}) collective-permute-start(f32[512,512]{1,0:T(8,128)} %pad_maximum_fusion.7), channel_id=1, source_target_pairs={{0,16},{4,20},{8,24},{12,28},{16,0},{20,4},{24,8},{28,12},{1,17},{... | collective-permute-start | bytes 3145736 | tf_op jit(solution)/shard_map/ppermute | solution.py:11
  574.2 73.3 %collective-permute-start.23 = (f32[512,512]{1,0:T(8,128)}, f32[512,512]{1,0:T(8,128)S(1)}, u32[]{:S(2)}, u32[]{:S(2)}) collective-permute-start(f32[512,512]{1,0:T(8,128)} %pad_maximum_fusion.11), channel_id=1, source_target_pairs={{0,16},{4,20},{8,24},{12,28},{16,0},{20,4},{24,8},{28,12},{1,17},{... | collective-permute-start | bytes 3145736 | tf_op jit(solution)/shard_map/ppermute | solution.py:11
  596.7 52.5 %collective-permute-start.22 = (f32[512,512]{1,0:T(8,128)}, f32[512,512]{1,0:T(8,128)S(1)}, u32[]{:S(2)}, u32[]{:S(2)}) collective-permute-start(f32[512,512]{1,0:T(8,128)} %pad_maximum_fusion.10), channel_id=1, source_target_pairs={{0,16},{4,20},{8,24},{12,28},{16,0},{20,4},{24,8},{28,12},{1,17},{... | collective-permute-start | bytes 3145736 | tf_op jit(solution)/shard_map/ppermute | solution.py:11
  619.2 32.6 %collective-permute-start = (f32[512,512]{1,0:T(8,128)S(1)}, f32[512,512]{1,0:T(8,128)S(1)}, u32[]{:S(2)}, u32[]{:S(2)}) collective-permute-start(f32[512,512]{1,0:T(8,128)S(1)} %copy-done.16), channel_id=1, source_target_pairs={{0,4},{4,0},{8,12},{12,8},{16,20},{20,16},{24,28},{28,24},{1,5},{5... | collective-permute-start | bytes 3145736 | tf_op jit(solution)/shard_map/ppermute | solution.py:11
  641.2 24.8 %collective-permute-start.6 = (f32[512,512]{1,0:T(8,128)S(1)}, f32[512,512]{1,0:T(8,128)S(1)}, u32[]{:S(2)}, u32[]{:S(2)}) collective-permute-start(f32[512,512]{1,0:T(8,128)S(1)} %copy-done.16), channel_id=1, source_target_pairs={{0,8},{4,12},{8,0},{12,4},{16,24},{20,28},{24,16},{28,20},{1,9},{5... | collective-permute-start | bytes 3145736 | tf_op jit(solution)/shard_map/ppermute | solution.py:11
  643.8 26.4 %collective-permute-start.21 = (f32[512,512]{1,0:T(8,128)}, f32[512,512]{1,0:T(8,128)S(1)}, u32[]{:S(2)}, u32[]{:S(2)}) collective-permute-start(f32[512,512]{1,0:T(8,128)} %pad_maximum_fusion.9), channel_id=1, source_target_pairs={{0,16},{4,20},{8,24},{12,28},{16,0},{20,4},{24,8},{28,12},{1,17},{... | collective-permute-start | bytes 3145736 | tf_op jit(solution)/shard_map/ppermute | solution.py:11
  647.6 45.1 %collective-permute-start.20 = (f32[512,512]{1,0:T(8,128)S(1)}, f32[512,512]{1,0:T(8,128)S(1)}, u32[]{:S(2)}, u32[]{:S(2)}) collective-permute-start(f32[512,512]{1,0:T(8,128)S(1)} %pad_maximum_fusion.8), channel_id=1, source_target_pairs={{0,16},{4,20},{8,24},{12,28},{16,0},{20,4},{24,8},{28,12},{1,17},{... | collective-permute-start | bytes 3145736 | tf_op jit(solution)/shard_map/ppermute | solution.py:11
  649.2 65.9 %collective-permute-start.18 = (f32[512,512]{1,0:T(8,128)S(1)}, f32[512,512]{1,0:T(8,128)S(1)}, u32[]{:S(2)}, u32[]{:S(2)}) collective-permute-start(f32[512,512]{1,0:T(8,128)S(1)} %copy-done.16), channel_id=1, source_target_pairs={{0,16},{4,20},{8,24},{12,28},{16,0},{20,4},{24,8},{28,12},{1,17},{... | collective-permute-start | bytes 3145736 | tf_op jit(solution)/shard_map/ppermute | solution.py:11
  651.8 74.5 %collective-permute-start.32 = (f32[256,512]{1,0:T(8,128)S(1)}, f32[256,512]{1,0:T(8,128)S(1)}, u32[]{:S(2)}, u32[]{:S(2)}) collective-permute-start(f32[256,512]{1,0:T(8,128)S(1)} %slice.176), channel_id=1, source_target_pairs={{0,16},{4,20},{8,24},{12,28},{16,0},{20,4},{24,8},{28,12},{1,17},{... | collective-permute-start | bytes 1572872 | tf_op jit(solution)/shard_map/ppermute | solution.py:11
  666.0 71.5 %collective-permute-start.40 = (f32[256,512]{1,0:T(8,128)S(1)}, f32[256,512]{1,0:T(8,128)S(1)}, u32[]{:S(2)}, u32[]{:S(2)}) collective-permute-start(f32[256,512]{1,0:T(8,128)S(1)} %slice.184), channel_id=1, source_target_pairs={{0,16},{4,20},{8,24},{12,28},{16,0},{20,4},{24,8},{28,12},{1,17},{... | collective-permute-start | bytes 1572872 | tf_op jit(solution)/shard_map/ppermute | solution.py:11
  670.1 78.6 %collective-permute-start.38 = (f32[256,512]{1,0:T(8,128)S(1)}, f32[256,512]{1,0:T(8,128)S(1)}, u32[]{:S(2)}, u32[]{:S(2)}) collective-permute-start(f32[256,512]{1,0:T(8,128)S(1)} %slice.182), channel_id=1, source_target_pairs={{0,16},{4,20},{8,24},{12,28},{16,0},{20,4},{24,8},{28,12},{1,17},{... | collective-permute-start | bytes 1572872 | tf_op jit(solution)/shard_map/ppermute | solution.py:11
  692.6 67.4 %collective-permute-start.36 = (f32[256,512]{1,0:T(8,128)S(1)}, f32[256,512]{1,0:T(8,128)S(1)}, u32[]{:S(2)}, u32[]{:S(2)}) collective-permute-start(f32[256,512]{1,0:T(8,128)S(1)} %slice.180), channel_id=1, source_target_pairs={{0,16},{4,20},{8,24},{12,28},{16,0},{20,4},{24,8},{28,12},{1,17},{... | collective-permute-start | bytes 1572872 | tf_op jit(solution)/shard_map/ppermute | solution.py:11
  715.1 56.2 %collective-permute-start.34 = (f32[256,512]{1,0:T(8,128)S(1)}, f32[256,512]{1,0:T(8,128)S(1)}, u32[]{:S(2)}, u32[]{:S(2)}) collective-permute-start(f32[256,512]{1,0:T(8,128)S(1)} %slice.178), channel_id=1, source_target_pairs={{0,16},{4,20},{8,24},{12,28},{16,0},{20,4},{24,8},{28,12},{1,17},{... | collective-permute-start | bytes 1572872 | tf_op jit(solution)/shard_map/ppermute | solution.py:11
  726.3 54.6 %collective-permute-start.30 = (f32[256,512]{1,0:T(8,128)S(1)}, f32[256,512]{1,0:T(8,128)S(1)}, u32[]{:S(2)}, u32[]{:S(2)}) collective-permute-start(f32[256,512]{1,0:T(8,128)S(1)} %slice.174), channel_id=1, source_target_pairs={{0,16},{4,20},{8,24},{12,28},{16,0},{20,4},{24,8},{28,12},{1,17},{... | collective-permute-start | bytes 1572872 | tf_op jit(solution)/shard_map/ppermute | solution.py:11
  737.6 44.0 %collective-permute-start.33 = (f32[256,512]{1,0:T(8,128)S(1)}, f32[256,512]{1,0:T(8,128)S(1)}, u32[]{:S(2)}, u32[]{:S(2)}) collective-permute-start(f32[256,512]{1,0:T(8,128)S(1)} %slice.177), channel_id=1, source_target_pairs={{0,8},{4,12},{8,0},{12,4},{16,24},{20,28},{24,16},{28,20},{1,9},{5... | collective-permute-start | bytes 1572872 | tf_op jit(solution)/shard_map/ppermute | solution.py:11
  748.8 34.3 %collective-permute-start.41 = (f32[256,512]{1,0:T(8,128)S(1)}, f32[256,512]{1,0:T(8,128)S(1)}, u32[]{:S(2)}, u32[]{:S(2)}) collective-permute-start(f32[256,512]{1,0:T(8,128)S(1)} %slice.185), channel_id=1, source_target_pairs={{0,8},{4,12},{8,0},{12,4},{16,24},{20,28},{24,16},{28,20},{1,9},{5... | collective-permute-start | bytes 1572872 | tf_op jit(solution)/shard_map/ppermute | solution.py:11
  760.0 23.2 %collective-permute-start.39 = (f32[256,512]{1,0:T(8,128)S(1)}, f32[256,512]{1,0:T(8,128)S(1)}, u32[]{:S(2)}, u32[]{:S(2)}) collective-permute-start(f32[256,512]{1,0:T(8,128)S(1)} %slice.183), channel_id=1, source_target_pairs={{0,8},{4,12},{8,0},{12,4},{16,24},{20,28},{24,16},{28,20},{1,9},{5... | collective-permute-start | bytes 1572872 | tf_op jit(solution)/shard_map/ppermute | solution.py:11
  771.3 12.6 %collective-permute-start.37 = (f32[256,512]{1,0:T(8,128)S(1)}, f32[256,512]{1,0:T(8,128)S(1)}, u32[]{:S(2)}, u32[]{:S(2)}) collective-permute-start(f32[256,512]{1,0:T(8,128)S(1)} %slice.181), channel_id=1, source_target_pairs={{0,8},{4,12},{8,0},{12,4},{16,24},{20,28},{24,16},{28,20},{1,9},{5... | collective-permute-start | bytes 1572872 | tf_op jit(solution)/shard_map/ppermute | solution.py:11
  780.9 14.9 %collective-permute-start.35 = (f32[256,512]{1,0:T(8,128)S(1)}, f32[256,512]{1,0:T(8,128)S(1)}, u32[]{:S(2)}, u32[]{:S(2)}) collective-permute-start(f32[256,512]{1,0:T(8,128)S(1)} %slice.179), channel_id=1, source_target_pairs={{0,8},{4,12},{8,0},{12,4},{16,24},{20,28},{24,16},{28,20},{1,9},{5... | collective-permute-start | bytes 1572872 | tf_op jit(solution)/shard_map/ppermute | solution.py:11
  781.5 23.0 %collective-permute-start.31 = (f32[256,512]{1,0:T(8,128)S(1)}, f32[256,512]{1,0:T(8,128)S(1)}, u32[]{:S(2)}, u32[]{:S(2)}) collective-permute-start(f32[256,512]{1,0:T(8,128)S(1)} %slice.175), channel_id=1, source_target_pairs={{0,8},{4,12},{8,0},{12,4},{16,24},{20,28},{24,16},{28,20},{1,9},{5... | collective-permute-start | bytes 1572872 | tf_op jit(solution)/shard_map/ppermute | solution.py:11
  783.1 25.6 %collective-permute-start.13 = (f32[512,512]{1,0:T(8,128)}, f32[512,512]{1,0:T(8,128)S(1)}, u32[]{:S(2)}, u32[]{:S(2)}) collective-permute-start(f32[512,512]{1,0:T(8,128)} %collective-permute-done.7), channel_id=1, source_target_pairs={{0,4},{4,0},{8,12},{12,8},{16,20},{20,16},{24,28},{28,24},{1,5},{5... | collective-permute-start | bytes 3145736 | tf_op jit(solution)/shard_map/ppermute | solution.py:11
  783.2 27.1 %collective-permute-start.17 = (f32[512,512]{1,0:T(8,128)S(1)}, f32[512,512]{1,0:T(8,128)S(1)}, u32[]{:S(2)}, u32[]{:S(2)}) collective-permute-start(f32[512,512]{1,0:T(8,128)S(1)} %collective-permute-done.11), channel_id=1, source_target_pairs={{0,4},{4,0},{8,12},{12,8},{16,20},{20,16},{24,28},{28,24},{1,5},{5... | collective-permute-start | bytes 3145736 | tf_op jit(solution)/shard_map/ppermute | solution.py:11
  783.8 27.9 %collective-permute-start.16 = (f32[512,512]{1,0:T(8,128)S(1)}, f32[512,512]{1,0:T(8,128)S(1)}, u32[]{:S(2)}, u32[]{:S(2)}) collective-permute-start(f32[512,512]{1,0:T(8,128)S(1)} %collective-permute-done.10), channel_id=1, source_target_pairs={{0,4},{4,0},{8,12},{12,8},{16,20},{20,16},{24,28},{28,24},{1,5},{5... | collective-permute-start | bytes 3145736 | tf_op jit(solution)/shard_map/ppermute | solution.py:11
  795.8 17.5 %collective-permute-start.15 = (f32[512,512]{1,0:T(8,128)S(1)}, f32[512,512]{1,0:T(8,128)S(1)}, u32[]{:S(2)}, u32[]{:S(2)}) collective-permute-start(f32[512,512]{1,0:T(8,128)S(1)} %collective-permute-done.9), channel_id=1, source_target_pairs={{0,4},{4,0},{8,12},{12,8},{16,20},{20,16},{24,28},{28,24},{1,5},{5... | collective-permute-start | bytes 3145736 | tf_op jit(solution)/shard_map/ppermute | solution.py:11
  808.7 12.7 %collective-permute-start.12 = (f32[512,512]{1,0:T(8,128)S(1)}, f32[512,512]{1,0:T(8,128)S(1)}, u32[]{:S(2)}, u32[]{:S(2)}) collective-permute-start(f32[512,512]{1,0:T(8,128)S(1)} %collective-permute-done.6), channel_id=1, source_target_pairs={{0,4},{4,0},{8,12},{12,8},{16,20},{20,16},{24,28},{28,24},{1,5},{5... | collective-permute-start | bytes 3145736 | tf_op jit(solution)/shard_map/ppermute | solution.py:11
  817.1 10.8 %collective-permute-start.24 = (f32[512,512]{1,0:T(8,128)S(1)}, f32[512,512]{1,0:T(8,128)S(1)}, u32[]{:S(2)}, u32[]{:S(2)}) collective-permute-start(f32[512,512]{1,0:T(8,128)S(1)} %collective-permute-done.18), channel_id=1, source_target_pairs={{0,4},{4,0},{8,12},{12,8},{16,20},{20,16},{24,28},{28,24},{1,5},{5... | collective-permute-start | bytes 3145736 | tf_op jit(solution)/shard_map/ppermute | solution.py:11
  818.7 13.9 %collective-permute-start.43 = (f32[512,512]{1,0:T(8,128)S(1)}, f32[512,512]{1,0:T(8,128)S(1)}, u32[]{:S(2)}, u32[]{:S(2)}) collective-permute-start(f32[512,512]{1,0:T(8,128)S(1)} %constant_dynamic-update-slice_fusion.2), channel_id=1, source_target_pairs={{0,4},{4,0},{8,12},{12,8},{16,20},{20,16},{24,28},{28,24},{1,5},{5... | collective-permute-start | bytes 3145736 | tf_op jit(solution)/shard_map/ppermute | solution.py:11
  819.9 14.3 %collective-permute-start.47 = (f32[512,512]{1,0:T(8,128)S(1)}, f32[512,512]{1,0:T(8,128)S(1)}, u32[]{:S(2)}, u32[]{:S(2)}) collective-permute-start(f32[512,512]{1,0:T(8,128)S(1)} %constant_dynamic-update-slice_fusion.10), channel_id=1, source_target_pairs={{0,4},{4,0},{8,12},{12,8},{16,20},{20,16},{24,28},{28,24},{1,5},{5... | collective-permute-start | bytes 3145736 | tf_op jit(solution)/shard_map/ppermute | solution.py:11
  821.4 13.8 %collective-permute-start.46 = (f32[512,512]{1,0:T(8,128)S(1)}, f32[512,512]{1,0:T(8,128)S(1)}, u32[]{:S(2)}, u32[]{:S(2)}) collective-permute-start(f32[512,512]{1,0:T(8,128)S(1)} %constant_dynamic-update-slice_fusion.8), channel_id=1, source_target_pairs={{0,4},{4,0},{8,12},{12,8},{16,20},{20,16},{24,28},{28,24},{1,5},{5... | collective-permute-start | bytes 3145736 | tf_op jit(solution)/shard_map/ppermute | solution.py:11
  826.1 10.2 %collective-permute-start.45 = (f32[512,512]{1,0:T(8,128)S(1)}, f32[512,512]{1,0:T(8,128)S(1)}, u32[]{:S(2)}, u32[]{:S(2)}) collective-permute-start(f32[512,512]{1,0:T(8,128)S(1)} %constant_dynamic-update-slice_fusion.6), channel_id=1, source_target_pairs={{0,4},{4,0},{8,12},{12,8},{16,20},{20,16},{24,28},{28,24},{1,5},{5... | collective-permute-start | bytes 3145736 | tf_op jit(solution)/shard_map/ppermute | solution.py:11
  (25 other events, 174.3 us)
Sparse Core Ops, SparseCore 0:
  9.2 40.1 all-gather.1
  64.2 76.7 reduce-scatter.9
  143.4 77.2 reduce-scatter.17
  222.8 77.2 reduce-scatter.15
  302.3 77.2 reduce-scatter.13
  381.8 77.2 reduce-scatter.7
  461.5 77.2 reduce-scatter.11
  841.0 144.0 reduce-scatter.19

commit v2 on v1

--- a/solution.py
+++ b/solution.py
@@ -3,7 +3,7 @@
 from jax import lax
 from jax.sharding import PartitionSpec as P
 
-GROUPS = 6
+GROUPS = (2, 3, 3, 2, 1, 1)
 
 
 def exchanged(block, axis, flip):
@@ -43,20 +43,29 @@
     blk_size = lax.axis_size("blk")
     place = lax.axis_index("blk")
     orbitals = lax.all_gather(coefficients, "blk", axis=1, tiled=True)
-    per_group = aux_count // GROUPS
     tiles = None
-    for group in range(GROUPS):
-        part = three_index[:, group * per_group : (group + 1) * per_group]
+    earlier = []
+    begin = 0
+    for per_group in GROUPS:
+        part = three_index[:, begin : begin + per_group]
+        begin += per_group
         partial_x = jnp.concatenate(
             [product(part[:, p], orbitals, ((1,), (0,))) for p in range(per_group)], axis=0
         )
+        if len(earlier) >= 2:
+            partial_x, earlier[-2] = lax.optimization_barrier((partial_x, earlier[-2]))
         half_x = lax.psum_scatter(partial_x, "col", scatter_dimension=1, tiled=True)
+        if len(earlier) >= 2:
+            tiles = [t + u for t, u in zip(tiles, earlier[-2])] if tiles else earlier[-2]
+        if earlier:
+            half_x, earlier[-1] = lax.optimization_barrier((half_x, earlier[-1]))
         own = jnp.concatenate(
             [half_x[p * row_count : (p + 1) * row_count] for p in range(per_group)], axis=1
         )
         blocks = blocks_of_others(own, "blk")
-        terms = [product(own, block, ((1,), (1,))) for block in blocks]
-        tiles = terms if tiles is None else [t + u for t, u in zip(tiles, terms)]
+        earlier.append([product(own, block, ((1,), (1,))) for block in blocks])
+    for terms in earlier[-2:]:
+        tiles = [t + u for t, u in zip(tiles, terms)]
     exchange_part = jnp.concatenate(tiles, axis=1)
     rows = lax.psum_scatter(exchange_part, "col", scatter_dimension=0, tiled=True)
     shares = jnp.split(rows, blk_size, axis=1)

time: 1010 us -> 753 us (0.75)
  waiting for transfers between devices: 771 us -> 460 us
  matrix products: 139 us -> 189 us
  local copies, waits for them, and re-layouts: 14.1 us -> 25.1 us
  other arithmetic: 30.3 us -> 19.8 us
    reduce_scatter x6, waiting for transfers between devices: 382 us -> 149 us  [on_device(): half_x = lax.psum_scatter(partial_x, 'col', scatter_dimension=1, tiled=True)]
    ppermute x48, waiting for transfers between devices: 202 us -> 125 us  [exchanged(): return lax.ppermute(block, axis, route)]
    dot_general x60, matrix products: 139 us -> 189 us  [product(): lax.dot_general(left, right, (dims, ((), ())), precision=lax.Precision.HI...]
  transfers between devices with their start and end apart: 56 -> 56, of which waited for: 24 -> 22; matrix products, arithmetic and copies ran while one was open for 15% -> 28% of each run, Pallas kernels for 0% -> 0%
where the time goes in v2:
time: 753 us; the launch traced here: 748 us
  waiting for transfers between devices  460 us (61%)
  matrix products  189 us (25%)
  starting transfers between devices  38.6 us (5%)
  local copies, waits for them, and re-layouts  25.1 us (3%)
  other arithmetic  19.8 us (3%)
  between operations  14.5 us (2%)
    dot_general x60, matrix products, product(): lax.dot_general(left, right, (dims, ((), ())), precision=lax.Precision.HI...  189 us
    reduce_scatter x6, waiting for transfers between devices, on_device(): half_x = lax.psum_scatter(partial_x, 'col', scatter_dimension=1, tiled=True)  149 us
    reduce_scatter x1, waiting for transfers between devices, on_device(): lax.psum_scatter(exchange_part, 'col', scatter_dimension=0, tiled=True)  143 us
    ppermute x48, waiting for transfers between devices, exchanged(): return lax.ppermute(block, axis, route)  125 us
    all_gather x1, waiting for transfers between devices, on_device(): orbitals = lax.all_gather(coefficients, 'blk', axis=1, tiled=True)  42.1 us
    ppermute x48, starting transfers between devices, exchanged(): return lax.ppermute(block, axis, route)  37.8 us
  transfers between devices with their start and end apart: 56, of which 22 were waited for; matrix products, arithmetic and copies ran while one was open for 28% of the time, Pallas kernels for 0%

profile of v2, /device:TPU:0, one launch (start us, length us, event | category | flops | bytes accessed | tf_op | source)
XLA Modules:
  0.0 747.6 jit_solution(1392696348014096477)
XLA Ops:
  7.3 42.1 %all-gather.2.cloned.1.call-done = f32[1024,1024]{1,0:T(8,128)} async-done(((f32[1024,128]{1,0:T(8,128)}), f32[1024,1024]{1,0:T(8,128)}) %all-gather.2.cloned.1.call-update) | async-done | bytes 4194320 | tf_op jit(solution)/shard_map/all_gather | solution.py:45
  49.4 6.5 fusion.8
  55.9 5.4 fusion.10
  61.3 2.6 pad_maximum_fusion.2
  64.1 6.5 fusion.12
  70.6 5.4 fusion.14
  76.0 5.4 fusion.16
  81.3 3.3 pad_maximum_fusion.1
  84.7 6.7 fusion.18
  91.4 49.3 %reduce-scatter.10.cloned.1.call-done = f32[1024,256]{1,0:T(8,128)} async-done(((f32[1024,1024]{1,0:T(8,128)}), f32[1024,256]{1,0:T(8,128)}) %reduce-scatter.10.cloned.1.call-update) | async-done | bytes 1048592 | tf_op jit(solution)/shard_map/reduce_scatter | solution.py:57
  146.3 5.4 fusion.20
  151.6 5.4 fusion.22
  157.1 3.3 pad_maximum_fusion
  162.4 6.2 collective-permute-done.1
  173.8 3.3 fusion.57
  179.9 2.6 collective-permute-done.5
  185.0 3.4 fusion.58
  196.5 57.9 %reduce-scatter.8.cloned.1.call-done = f32[1536,256]{1,0:T(8,128)} async-done(((f32[1536,1024]{1,0:T(8,128)}), f32[1536,256]{1,0:T(8,128)}) %reduce-scatter.8.cloned.1.call-update) | async-done | bytes 1572880 | tf_op jit(solution)/shard_map/reduce_scatter | solution.py:57
  260.3 5.4 fusion.4
  265.8 28.1 %collective-permute-done.9 = f32[512,768]{1,0:T(8,128)} collective-permute-done((f32[512,768]{1,0:T(8,128)}, f32[512,768]{1,0:T(8,128)}, u32[]{:S(2)}, u32[]{:S(2)}) %collective-permute-start.9) | collective-permute-done | bytes 1572896 | tf_op jit(solution)/shard_map/ppermute | solution.py:11
  299.9 5.4 fusion.6
  305.4 2.6 pad_maximum_fusion.3
  310.9 3.8 collective-permute-done.13
  318.3 3.8 fusion.73
  322.1 2.7 fusion.71
  324.8 3.9 fusion.74
  331.1 3.9 fusion.72
  337.4 2.5 fusion.68
  339.9 28.1 %reduce-scatter.12.cloned.1.call-done = f32[1536,256]{1,0:T(8,128)} async-done(((f32[1536,1024]{1,0:T(8,128)}), f32[1536,256]{1,0:T(8,128)}) %reduce-scatter.12.cloned.1.call-update) | async-done | bytes 1572880 | tf_op jit(solution)/shard_map/reduce_scatter | solution.py:57
  374.2 33.6 %collective-permute-done.17 = f32[512,768]{1,0:T(8,128)} collective-permute-done((f32[512,768]{1,0:T(8,128)}, f32[512,768]{1,0:T(8,128)}, u32[]{:S(2)}, u32[]{:S(2)}) %collective-permute-start.17) | collective-permute-done | bytes 1572896 | tf_op jit(solution)/shard_map/ppermute | solution.py:11
  415.0 6.6 fusion.2
  424.4 4.1 collective-permute-done.21
  428.5 5.1 collective-permute-done.22
  434.9 3.8 fusion.65
  441.1 3.8 fusion.66
  447.5 4.0 fusion.64
  451.5 2.6 fusion.62
  461.2 6.9 fusion
  470.1 15.0 %collective-permute-done.25 = f32[512,512]{1,0:T(8,128)} collective-permute-done((f32[512,512]{1,0:T(8,128)}, f32[512,512]{1,0:T(8,128)}, u32[]{:S(2)}, u32[]{:S(2)}) %collective-permute-start.25) | collective-permute-done | bytes 1048608 | tf_op jit(solution)/shard_map/ppermute | solution.py:11
  489.4 3.3 fusion.49
  493.2 3.2 fusion.47
  496.4 3.3 collective-permute-done.29
  501.3 3.2 fusion.50
  518.4 9.8 %collective-permute-done.33 = f32[512,256]{1,0:T(8,128)S(1)} collective-permute-done((f32[512,256]{1,0:T(8,128)S(1)}, f32[512,256]{1,0:T(8,128)S(1)}, u32[]{:S(2)}, u32[]{:S(2)}) %collective-permute-start.33) | collective-permute-done | bytes 524320 | tf_op jit(solution)/shard_map/ppermute | solution.py:11
  544.2 13.3 %reduce-scatter.18.cloned.1.call-done = f32[512,256]{1,0:T(8,128)} async-done(((f32[512,1024]{1,0:T(8,128)}), f32[512,256]{1,0:T(8,128)}) %reduce-scatter.18.cloned.1.call-update) | async-done | bytes 524304 | tf_op jit(solution)/shard_map/reduce_scatter | solution.py:57
  560.6 4.6 fusion.43
  565.2 6.2 collective-permute-done.41
  592.0 143.5 %reduce-scatter.20.cloned.1.call-done = f32[128,4096]{1,0:T(8,128)} async-done(((f32[512,4096]{1,0:T(8,128)}), f32[128,4096]{1,0:T(8,128)}) %reduce-scatter.20.cloned.1.call-update) | async-done | bytes 2097168 | tf_op jit(solution)/shard_map/reduce_scatter | solution.py:70
  (272 shorter events, 146.6 us)
Async XLA Ops:
  6.5 42.9 %all-gather.2.cloned.1.call-start = ((), (), s32[]{:S(2)}) async-start(), calls=%async_computation.7 | async-start | bytes 4718592 | tf_op jit(solution)/shard_map/all_gather | solution.py:45
  7.3 133.5 %reduce-scatter.10.cloned.1.call-start = ((), (), s32[]{:S(2)}) async-start(), calls=%async_computation.9 | async-start | bytes 5242880 | tf_op jit(solution)/shard_map/reduce_scatter | solution.py:57
  63.8 190.6 %reduce-scatter.8.cloned.1.call-start = ((), (), s32[]{:S(2)}) async-start(), calls=%async_computation.8 | async-start | bytes 7864320 | tf_op jit(solution)/shard_map/reduce_scatter | solution.py:57
  84.6 283.4 %reduce-scatter.12.cloned.1.call-start = ((), (), s32[]{:S(2)}) async-start(), calls=%async_computation.10 | async-start | bytes 7864320 | tf_op jit(solution)/shard_map/reduce_scatter | solution.py:57
  143.3 25.2 %collective-permute-start.1 = (f32[512,512]{1,0:T(8,128)}, f32[512,512]{1,0:T(8,128)}, u32[]{:S(2)}, u32[]{:S(2)}) collective-permute-start(f32[512,512]{1,0:T(8,128)} %pad_maximum_fusion.6), channel_id=1, source_target_pairs={{0,8},{4,12},{8,0},{12,4},{16,24},{20,28},{24,16},{28,20},{1,9},{5... | collective-permute-start | bytes 3145736 | tf_op jit(solution)/shard_map/ppermute | solution.py:11
  144.8 26.4 %collective-permute-start.3 = (f32[512,512]{1,0:T(8,128)}, f32[512,512]{1,0:T(8,128)}, u32[]{:S(2)}, u32[]{:S(2)}) collective-permute-start(f32[512,512]{1,0:T(8,128)} %pad_maximum_fusion.6), channel_id=1, source_target_pairs={{0,16},{4,20},{8,24},{12,28},{16,0},{20,4},{24,8},{28,12},{1,17},{... | collective-permute-start | bytes 3145736 | tf_op jit(solution)/shard_map/ppermute | solution.py:11
  157.0 28.0 %collective-permute-start = (f32[512,512]{1,0:T(8,128)}, f32[512,512]{1,0:T(8,128)}, u32[]{:S(2)}, u32[]{:S(2)}) collective-permute-start(f32[512,512]{1,0:T(8,128)} %pad_maximum_fusion.6), channel_id=1, source_target_pairs={{0,4},{4,0},{8,12},{12,8},{16,20},{20,16},{24,28},{28,24},{1,5},{5... | collective-permute-start | bytes 3145736 | tf_op jit(solution)/shard_map/ppermute | solution.py:11
  169.6 12.9 %collective-permute-start.5 = (f32[256,512]{1,0:T(8,128)S(1)}, f32[256,512]{1,0:T(8,128)S(1)}, u32[]{:S(2)}, u32[]{:S(2)}) collective-permute-start(f32[256,512]{1,0:T(8,128)S(1)} %slice.152), channel_id=1, source_target_pairs={{0,16},{4,20},{8,24},{12,28},{16,0},{20,4},{24,8},{28,12},{1,17},{... | collective-permute-start | bytes 1572872 | tf_op jit(solution)/shard_map/ppermute | solution.py:11
  172.2 12.6 %collective-permute-start.6 = (f32[256,512]{1,0:T(8,128)S(1)}, f32[256,512]{1,0:T(8,128)S(1)}, u32[]{:S(2)}, u32[]{:S(2)}) collective-permute-start(f32[256,512]{1,0:T(8,128)S(1)} %slice.153), channel_id=1, source_target_pairs={{0,8},{4,12},{8,0},{12,4},{16,24},{20,28},{24,16},{28,20},{1,9},{5... | collective-permute-start | bytes 1572872 | tf_op jit(solution)/shard_map/ppermute | solution.py:11
  177.1 13.3 %collective-permute-start.2 = (f32[512,512]{1,0:T(8,128)}, f32[512,512]{1,0:T(8,128)S(1)}, u32[]{:S(2)}, u32[]{:S(2)}) collective-permute-start(f32[512,512]{1,0:T(8,128)} %collective-permute-done.1), channel_id=1, source_target_pairs={{0,4},{4,0},{8,12},{12,8},{16,20},{20,16},{24,28},{28,24},{1,5},{5... | collective-permute-start | bytes 3145736 | tf_op jit(solution)/shard_map/ppermute | solution.py:11
  177.1 15.3 %collective-permute-start.4 = (f32[512,512]{1,0:T(8,128)}, f32[512,512]{1,0:T(8,128)S(1)}, u32[]{:S(2)}, u32[]{:S(2)}) collective-permute-start(f32[512,512]{1,0:T(8,128)} %collective-permute-done.3), channel_id=1, source_target_pairs={{0,4},{4,0},{8,12},{12,8},{16,20},{20,16},{24,28},{28,24},{1,5},{5... | collective-permute-start | bytes 3145736 | tf_op jit(solution)/shard_map/ppermute | solution.py:11
  184.9 9.6 %collective-permute-start.7 = (f32[512,512]{1,0:T(8,128)S(1)}, f32[512,512]{1,0:T(8,128)S(1)}, u32[]{:S(2)}, u32[]{:S(2)}) collective-permute-start(f32[512,512]{1,0:T(8,128)S(1)} %constant_dynamic-update-slice_fusion), channel_id=1, source_target_pairs={{0,4},{4,0},{8,12},{12,8},{16,20},{20,16},{24,28},{28,24},{1,5},{5... | collective-permute-start | bytes 3145736 | tf_op jit(solution)/shard_map/ppermute | solution.py:11
  254.5 202.1 %reduce-scatter.14.cloned.1.call-start = ((), (), s32[]{:S(2)}) async-start(), calls=%async_computation.11 | async-start | bytes 5242880 | tf_op jit(solution)/shard_map/reduce_scatter | solution.py:57
  257.4 36.5 %collective-permute-start.9 = (f32[512,768]{1,0:T(8,128)}, f32[512,768]{1,0:T(8,128)}, u32[]{:S(2)}, u32[]{:S(2)}) collective-permute-start(f32[512,768]{1,0:T(8,128)} %pad_maximum_fusion.4), channel_id=1, source_target_pairs={{0,8},{4,12},{8,0},{12,4},{16,24},{20,28},{24,16},{28,20},{1,9},{5... | collective-permute-start | bytes 4718600 | tf_op jit(solution)/shard_map/ppermute | solution.py:11
  258.9 38.6 %collective-permute-start.11 = (f32[512,768]{1,0:T(8,128)}, f32[512,768]{1,0:T(8,128)S(1)}, u32[]{:S(2)}, u32[]{:S(2)}) collective-permute-start(f32[512,768]{1,0:T(8,128)} %pad_maximum_fusion.4), channel_id=1, source_target_pairs={{0,16},{4,20},{8,24},{12,28},{16,0},{20,4},{24,8},{28,12},{1,17},{... | collective-permute-start | bytes 4718600 | tf_op jit(solution)/shard_map/ppermute | solution.py:11
  265.7 59.1 %collective-permute-start.8 = (f32[512,768]{1,0:T(8,128)}, f32[512,768]{1,0:T(8,128)}, u32[]{:S(2)}, u32[]{:S(2)}) collective-permute-start(f32[512,768]{1,0:T(8,128)} %pad_maximum_fusion.4), channel_id=1, source_target_pairs={{0,4},{4,0},{8,12},{12,8},{16,20},{20,16},{24,28},{28,24},{1,5},{5... | collective-permute-start | bytes 4718600 | tf_op jit(solution)/shard_map/ppermute | solution.py:11
  296.0 18.7 %collective-permute-start.13 = (f32[256,768]{1,0:T(8,128)}, f32[256,768]{1,0:T(8,128)S(1)}, u32[]{:S(2)}, u32[]{:S(2)}) collective-permute-start(f32[256,768]{1,0:T(8,128)} %slice.154), channel_id=1, source_target_pairs={{0,16},{4,20},{8,24},{12,28},{16,0},{20,4},{24,8},{28,12},{1,17},{... | collective-permute-start | bytes 2359304 | tf_op jit(solution)/shard_map/ppermute | solution.py:11
  298.5 18.5 %collective-permute-start.14 = (f32[256,768]{1,0:T(8,128)}, f32[256,768]{1,0:T(8,128)}, u32[]{:S(2)}, u32[]{:S(2)}) collective-permute-start(f32[256,768]{1,0:T(8,128)} %slice.155), channel_id=1, source_target_pairs={{0,8},{4,12},{8,0},{12,4},{16,24},{20,28},{24,16},{28,20},{1,9},{5... | collective-permute-start | bytes 2359304 | tf_op jit(solution)/shard_map/ppermute | solution.py:11
  305.3 25.8 %collective-permute-start.10 = (f32[512,768]{1,0:T(8,128)}, f32[512,768]{1,0:T(8,128)}, u32[]{:S(2)}, u32[]{:S(2)}) collective-permute-start(f32[512,768]{1,0:T(8,128)} %collective-permute-done.9), channel_id=1, source_target_pairs={{0,4},{4,0},{8,12},{12,8},{16,20},{20,16},{24,28},{28,24},{1,5},{5... | collective-permute-start | bytes 4718600 | tf_op jit(solution)/shard_map/ppermute | solution.py:11
  310.4 24.5 %collective-permute-start.12 = (f32[512,768]{1,0:T(8,128)S(1)}, f32[512,768]{1,0:T(8,128)S(1)}, u32[]{:S(2)}, u32[]{:S(2)}) collective-permute-start(f32[512,768]{1,0:T(8,128)S(1)} %copy-done.44), channel_id=1, source_target_pairs={{0,4},{4,0},{8,12},{12,8},{16,20},{20,16},{24,28},{28,24},{1,5},{5... | collective-permute-start | bytes 4718600 | tf_op jit(solution)/shard_map/ppermute | solution.py:11
  318.2 19.3 %collective-permute-start.15 = (f32[512,768]{1,0:T(8,128)S(1)}, f32[512,768]{1,0:T(8,128)S(1)}, u32[]{:S(2)}, u32[]{:S(2)}) collective-permute-start(f32[512,768]{1,0:T(8,128)S(1)} %constant_dynamic-update-slice_fusion.2), channel_id=1, source_target_pairs={{0,4},{4,0},{8,12},{12,8},{16,20},{20,16},{24,28},{28,24},{1,5},{5... | collective-permute-start | bytes 4718600 | tf_op jit(solution)/shard_map/ppermute | solution.py:11
  368.0 144.8 %reduce-scatter.16.cloned.1.call-start = ((), (), s32[]{:S(2)}) async-start(), calls=%async_computation.12 | async-start | bytes 2621440 | tf_op jit(solution)/shard_map/reduce_scatter | solution.py:57
  371.2 36.5 %collective-permute-start.17 = (f32[512,768]{1,0:T(8,128)}, f32[512,768]{1,0:T(8,128)}, u32[]{:S(2)}, u32[]{:S(2)}) collective-permute-start(f32[512,768]{1,0:T(8,128)} %pad_maximum_fusion.5), channel_id=1, source_target_pairs={{0,8},{4,12},{8,0},{12,4},{16,24},{20,28},{24,16},{28,20},{1,9},{5... | collective-permute-start | bytes 4718600 | tf_op jit(solution)/shard_map/ppermute | solution.py:11
  372.7 38.6 %collective-permute-start.19 = (f32[512,768]{1,0:T(8,128)}, f32[512,768]{1,0:T(8,128)S(1)}, u32[]{:S(2)}, u32[]{:S(2)}) collective-permute-start(f32[512,768]{1,0:T(8,128)} %pad_maximum_fusion.5), channel_id=1, source_target_pairs={{0,16},{4,20},{8,24},{12,28},{16,0},{20,4},{24,8},{28,12},{1,17},{... | collective-permute-start | bytes 4718600 | tf_op jit(solution)/shard_map/ppermute | solution.py:11
  409.8 18.7 %collective-permute-start.21 = (f32[256,768]{1,0:T(8,128)}, f32[256,768]{1,0:T(8,128)S(1)}, u32[]{:S(2)}, u32[]{:S(2)}) collective-permute-start(f32[256,768]{1,0:T(8,128)} %slice.156), channel_id=1, source_target_pairs={{0,16},{4,20},{8,24},{12,28},{16,0},{20,4},{24,8},{28,12},{1,17},{... | collective-permute-start | bytes 2359304 | tf_op jit(solution)/shard_map/ppermute | solution.py:11
  411.2 29.9 %collective-permute-start.16 = (f32[512,768]{1,0:T(8,128)}, f32[512,768]{1,0:T(8,128)}, u32[]{:S(2)}, u32[]{:S(2)}) collective-permute-start(f32[512,768]{1,0:T(8,128)} %pad_maximum_fusion.5), channel_id=1, source_target_pairs={{0,4},{4,0},{8,12},{12,8},{16,20},{20,16},{24,28},{28,24},{1,5},{5... | collective-permute-start | bytes 4718600 | tf_op jit(solution)/shard_map/ppermute | solution.py:11
  413.3 20.3 %collective-permute-start.22 = (f32[256,768]{1,0:T(8,128)}, f32[256,768]{1,0:T(8,128)}, u32[]{:S(2)}, u32[]{:S(2)}) collective-permute-start(f32[256,768]{1,0:T(8,128)} %slice.157), channel_id=1, source_target_pairs={{0,8},{4,12},{8,0},{12,4},{16,24},{20,28},{24,16},{28,20},{1,9},{5... | collective-permute-start | bytes 2359304 | tf_op jit(solution)/shard_map/ppermute | solution.py:11
  414.8 32.7 %collective-permute-start.18 = (f32[512,768]{1,0:T(8,128)}, f32[512,768]{1,0:T(8,128)}, u32[]{:S(2)}, u32[]{:S(2)}) collective-permute-start(f32[512,768]{1,0:T(8,128)} %collective-permute-done.17), channel_id=1, source_target_pairs={{0,4},{4,0},{8,12},{12,8},{16,20},{20,16},{24,28},{28,24},{1,5},{5... | collective-permute-start | bytes 4718600 | tf_op jit(solution)/shard_map/ppermute | solution.py:11
  424.1 27.4 %collective-permute-start.20 = (f32[512,768]{1,0:T(8,128)S(1)}, f32[512,768]{1,0:T(8,128)S(1)}, u32[]{:S(2)}, u32[]{:S(2)}) collective-permute-start(f32[512,768]{1,0:T(8,128)S(1)} %copy-done.46), channel_id=1, source_target_pairs={{0,4},{4,0},{8,12},{12,8},{16,20},{20,16},{24,28},{28,24},{1,5},{5... | collective-permute-start | bytes 4718600 | tf_op jit(solution)/shard_map/ppermute | solution.py:11
  434.8 19.3 %collective-permute-start.23 = (f32[512,768]{1,0:T(8,128)S(1)}, f32[512,768]{1,0:T(8,128)S(1)}, u32[]{:S(2)}, u32[]{:S(2)}) collective-permute-start(f32[512,768]{1,0:T(8,128)S(1)} %constant_dynamic-update-slice_fusion.4), channel_id=1, source_target_pairs={{0,4},{4,0},{8,12},{12,8},{16,20},{20,16},{24,28},{28,24},{1,5},{5... | collective-permute-start | bytes 4718600 | tf_op jit(solution)/shard_map/ppermute | solution.py:11
  456.6 101.0 %reduce-scatter.18.cloned.1.call-start = ((), (), s32[]{:S(2)}) async-start(), calls=%async_computation.13 | async-start | bytes 2621440 | tf_op jit(solution)/shard_map/reduce_scatter | solution.py:57
  459.1 25.9 %collective-permute-start.25 = (f32[512,512]{1,0:T(8,128)}, f32[512,512]{1,0:T(8,128)}, u32[]{:S(2)}, u32[]{:S(2)}) collective-permute-start(f32[512,512]{1,0:T(8,128)} %pad_maximum_fusion.7), channel_id=1, source_target_pairs={{0,8},{4,12},{8,0},{12,4},{16,24},{20,28},{24,16},{28,20},{1,9},{5... | collective-permute-start | bytes 3145736 | tf_op jit(solution)/shard_map/ppermute | solution.py:11
  460.6 26.1 %collective-permute-start.27 = (f32[512,512]{1,0:T(8,128)}, f32[512,512]{1,0:T(8,128)}, u32[]{:S(2)}, u32[]{:S(2)}) collective-permute-start(f32[512,512]{1,0:T(8,128)} %pad_maximum_fusion.7), channel_id=1, source_target_pairs={{0,16},{4,20},{8,24},{12,28},{16,0},{20,4},{24,8},{28,12},{1,17},{... | collective-permute-start | bytes 3145736 | tf_op jit(solution)/shard_map/ppermute | solution.py:11
  461.2 40.1 %collective-permute-start.24 = (f32[512,512]{1,0:T(8,128)}, f32[512,512]{1,0:T(8,128)}, u32[]{:S(2)}, u32[]{:S(2)}) collective-permute-start(f32[512,512]{1,0:T(8,128)} %pad_maximum_fusion.7), channel_id=1, source_target_pairs={{0,4},{4,0},{8,12},{12,8},{16,20},{20,16},{24,28},{28,24},{1,5},{5... | collective-permute-start | bytes 3145736 | tf_op jit(solution)/shard_map/ppermute | solution.py:11
  486.1 13.6 %collective-permute-start.29 = (f32[256,512]{1,0:T(8,128)S(1)}, f32[256,512]{1,0:T(8,128)S(1)}, u32[]{:S(2)}, u32[]{:S(2)}) collective-permute-start(f32[256,512]{1,0:T(8,128)S(1)} %slice.158), channel_id=1, source_target_pairs={{0,16},{4,20},{8,24},{12,28},{16,0},{20,4},{24,8},{28,12},{1,17},{... | collective-permute-start | bytes 1572872 | tf_op jit(solution)/shard_map/ppermute | solution.py:11
  487.8 13.3 %collective-permute-start.30 = (f32[256,512]{1,0:T(8,128)S(1)}, f32[256,512]{1,0:T(8,128)S(1)}, u32[]{:S(2)}, u32[]{:S(2)}) collective-permute-start(f32[256,512]{1,0:T(8,128)S(1)} %slice.159), channel_id=1, source_target_pairs={{0,8},{4,12},{8,0},{12,4},{16,24},{20,28},{24,16},{28,20},{1,9},{5... | collective-permute-start | bytes 1572872 | tf_op jit(solution)/shard_map/ppermute | solution.py:11
  492.7 13.9 %collective-permute-start.26 = (f32[512,512]{1,0:T(8,128)}, f32[512,512]{1,0:T(8,128)S(1)}, u32[]{:S(2)}, u32[]{:S(2)}) collective-permute-start(f32[512,512]{1,0:T(8,128)} %collective-permute-done.25), channel_id=1, source_target_pairs={{0,4},{4,0},{8,12},{12,8},{16,20},{20,16},{24,28},{28,24},{1,5},{5... | collective-permute-start | bytes 3145736 | tf_op jit(solution)/shard_map/ppermute | solution.py:11
  492.7 15.9 %collective-permute-start.28 = (f32[512,512]{1,0:T(8,128)}, f32[512,512]{1,0:T(8,128)S(1)}, u32[]{:S(2)}, u32[]{:S(2)}) collective-permute-start(f32[512,512]{1,0:T(8,128)} %collective-permute-done.27), channel_id=1, source_target_pairs={{0,4},{4,0},{8,12},{12,8},{16,20},{20,16},{24,28},{28,24},{1,5},{5... | collective-permute-start | bytes 3145736 | tf_op jit(solution)/shard_map/ppermute | solution.py:11
  501.2 9.4 %collective-permute-start.31 = (f32[512,512]{1,0:T(8,128)S(1)}, f32[512,512]{1,0:T(8,128)S(1)}, u32[]{:S(2)}, u32[]{:S(2)}) collective-permute-start(f32[512,512]{1,0:T(8,128)S(1)} %constant_dynamic-update-slice_fusion.6), channel_id=1, source_target_pairs={{0,4},{4,0},{8,12},{12,8},{16,20},{20,16},{24,28},{28,24},{1,5},{5... | collective-permute-start | bytes 3145736 | tf_op jit(solution)/shard_map/ppermute | solution.py:11
  512.9 222.6 %reduce-scatter.20.cloned.1.call-start = ((), (), s32[]{:S(2)}) async-start(), calls=%async_computation.14 | async-start | bytes 10485760 | tf_op jit(solution)/shard_map/reduce_scatter | solution.py:70
  513.9 14.3 %collective-permute-start.33 = (f32[512,256]{1,0:T(8,128)S(1)}, f32[512,256]{1,0:T(8,128)S(1)}, u32[]{:S(2)}, u32[]{:S(2)}) collective-permute-start(f32[512,256]{1,0:T(8,128)S(1)} %copy-done.7), channel_id=1, source_target_pairs={{0,8},{4,12},{8,0},{12,4},{16,24},{20,28},{24,16},{28,20},{1,9},{5... | collective-permute-start | bytes 1572872 | tf_op jit(solution)/shard_map/ppermute | solution.py:11
  515.4 14.4 %collective-permute-start.35 = (f32[512,256]{1,0:T(8,128)S(1)}, f32[512,256]{1,0:T(8,128)S(1)}, u32[]{:S(2)}, u32[]{:S(2)}) collective-permute-start(f32[512,256]{1,0:T(8,128)S(1)} %copy-done.7), channel_id=1, source_target_pairs={{0,16},{4,20},{8,24},{12,28},{16,0},{20,4},{24,8},{28,12},{1,17},{... | collective-permute-start | bytes 1572872 | tf_op jit(solution)/shard_map/ppermute | solution.py:11
  516.8 18.2 %collective-permute-start.32 = (f32[512,256]{1,0:T(8,128)S(1)}, f32[512,256]{1,0:T(8,128)S(1)}, u32[]{:S(2)}, u32[]{:S(2)}) collective-permute-start(f32[512,256]{1,0:T(8,128)S(1)} %copy-done.7), channel_id=1, source_target_pairs={{0,4},{4,0},{8,12},{12,8},{16,20},{20,16},{24,28},{28,24},{1,5},{5... | collective-permute-start | bytes 1572872 | tf_op jit(solution)/shard_map/ppermute | solution.py:11
  531.3 9.6 %collective-permute-start.36 = (f32[512,256]{1,0:T(8,128)S(1)}, f32[512,256]{1,0:T(8,128)S(1)}, u32[]{:S(2)}, u32[]{:S(2)}) collective-permute-start(f32[512,256]{1,0:T(8,128)S(1)} %collective-permute-done.35), channel_id=1, source_target_pairs={{0,4},{4,0},{8,12},{12,8},{16,20},{20,16},{24,28},{28,24},{1,5},{5... | collective-permute-start | bytes 1572872 | tf_op jit(solution)/shard_map/ppermute | solution.py:11
  557.5 13.8 %collective-permute-start.41 = (f32[512,256]{1,0:T(8,128)}, f32[512,256]{1,0:T(8,128)S(1)}, u32[]{:S(2)}, u32[]{:S(2)}) collective-permute-start(f32[512,256]{1,0:T(8,128)} %reduce-scatter.18.cloned.1.call-done), channel_id=1, source_target_pairs={{0,8},{4,12},{8,0},{12,4},{16,24},{20,28},{24,16},{28,20},{1,9},{5... | collective-permute-start | bytes 1572872 | tf_op jit(solution)/shard_map/ppermute | solution.py:11
  559.1 13.8 %collective-permute-start.43 = (f32[512,256]{1,0:T(8,128)}, f32[512,256]{1,0:T(8,128)S(1)}, u32[]{:S(2)}, u32[]{:S(2)}) collective-permute-start(f32[512,256]{1,0:T(8,128)} %reduce-scatter.18.cloned.1.call-done), channel_id=1, source_target_pairs={{0,16},{4,20},{8,24},{12,28},{16,0},{20,4},{24,8},{28,12},{1,17},{... | collective-permute-start | bytes 1572872 | tf_op jit(solution)/shard_map/ppermute | solution.py:11
  560.5 14.5 %collective-permute-start.40 = (f32[512,256]{1,0:T(8,128)}, f32[512,256]{1,0:T(8,128)S(1)}, u32[]{:S(2)}, u32[]{:S(2)}) collective-permute-start(f32[512,256]{1,0:T(8,128)} %reduce-scatter.18.cloned.1.call-done), channel_id=1, source_target_pairs={{0,4},{4,0},{8,12},{12,8},{16,20},{20,16},{24,28},{28,24},{1,5},{5... | collective-permute-start | bytes 1572872 | tf_op jit(solution)/shard_map/ppermute | solution.py:11
  574.5 9.8 %collective-permute-start.44 = (f32[512,256]{1,0:T(8,128)S(1)}, f32[512,256]{1,0:T(8,128)S(1)}, u32[]{:S(2)}, u32[]{:S(2)}) collective-permute-start(f32[512,256]{1,0:T(8,128)S(1)} %collective-permute-done.43), channel_id=1, source_target_pairs={{0,4},{4,0},{8,12},{12,8},{16,20},{20,16},{24,28},{28,24},{1,5},{5... | collective-permute-start | bytes 1572872 | tf_op jit(solution)/shard_map/ppermute | solution.py:11
  (56 other events, 349.3 us)
Sparse Core Ops, SparseCore 0:
  9.2 40.1 all-gather.1
  64.0 76.7 reduce-scatter.9
  143.2 111.2 reduce-scatter.7
  256.7 111.2 reduce-scatter.11
  370.3 77.2 reduce-scatter.13
  456.7 43.6 reduce-scatter.15
  513.0 44.4 reduce-scatter.17
  592.1 143.3 reduce-scatter.19

commit v3 on v2

--- a/solution.py
+++ b/solution.py
@@ -3,7 +3,7 @@
 from jax import lax
 from jax.sharding import PartitionSpec as P
 
-GROUPS = (2, 3, 3, 2, 1, 1)
+GROUPS = (1, 3, 3, 2, 1, 1, 1)
 
 
 def exchanged(block, axis, flip):
@@ -42,7 +42,10 @@
     row_count, aux_count, _ = three_index.shape
     blk_size = lax.axis_size("blk")
     place = lax.axis_index("blk")
-    orbitals = lax.all_gather(coefficients, "blk", axis=1, tiled=True)
+    width = coefficients.shape[1]
+    orbitals = jnp.zeros((coefficients.shape[0], width * blk_size), jnp.float32)
+    for j, block in enumerate(blocks_of_others(coefficients, "blk")):
+        orbitals = lax.dynamic_update_slice(orbitals, block, (0, (place ^ j) * width))
     tiles = None
     earlier = []
     begin = 0
@@ -52,11 +55,11 @@
         partial_x = jnp.concatenate(
             [product(part[:, p], orbitals, ((1,), (0,))) for p in range(per_group)], axis=0
         )
-        if len(earlier) >= 2:
-            partial_x, earlier[-2] = lax.optimization_barrier((partial_x, earlier[-2]))
+        if len(earlier) >= 3:
+            partial_x, earlier[-3] = lax.optimization_barrier((partial_x, earlier[-3]))
         half_x = lax.psum_scatter(partial_x, "col", scatter_dimension=1, tiled=True)
-        if len(earlier) >= 2:
-            tiles = [t + u for t, u in zip(tiles, earlier[-2])] if tiles else earlier[-2]
+        if len(earlier) >= 3:
+            tiles = [t + u for t, u in zip(tiles, earlier[-3])] if tiles else earlier[-3]
         if earlier:
             half_x, earlier[-1] = lax.optimization_barrier((half_x, earlier[-1]))
         own = jnp.concatenate(
@@ -64,7 +67,7 @@
         )
         blocks = blocks_of_others(own, "blk")
         earlier.append([product(own, block, ((1,), (1,))) for block in blocks])
-    for terms in earlier[-2:]:
+    for terms in earlier[-3:]:
         tiles = [t + u for t, u in zip(tiles, terms)]
     exchange_part = jnp.concatenate(tiles, axis=1)
     rows = lax.psum_scatter(exchange_part, "col", scatter_dimension=0, tiled=True)

time: 753 us -> 733 us (0.973)
  waiting for transfers between devices: 460 us -> 407 us
  matrix products: 189 us -> 213 us
  starting transfers between devices: 38.6 us -> 50.7 us
    all_gather x1 -> x0, waiting for transfers between devices: 42.1 us -> none  [on_device(): orbitals = lax.all_gather(coefficients, 'blk', axis=1, tiled=True)]
    dot_general x60 -> x68, matrix products: 189 us -> 213 us  [product(): lax.dot_general(left, right, (dims, ((), ())), precision=lax.Precision.HI...]
    reduce_scatter x6 -> x7, waiting for transfers between devices: 149 us -> 130 us  [on_device(): half_x = lax.psum_scatter(partial_x, 'col', scatter_dimension=1, tiled=True)]
    ppermute x48 -> x64, starting transfers between devices: 37.8 us -> 48.9 us  [exchanged(): return lax.ppermute(block, axis, route)]
    ppermute x48 -> x64, waiting for transfers between devices: 125 us -> 134 us  [exchanged(): return lax.ppermute(block, axis, route)]
  transfers between devices with their start and end apart: 56 -> 72, of which waited for: 22 -> 22; matrix products, arithmetic and copies ran while one was open for 28% -> 32% of each run, Pallas kernels for 0% -> 0%
where the time goes in v3:
time: 733 us; the launch traced here: 726 us
  waiting for transfers between devices  407 us (56%)
  matrix products  213 us (29%)
  starting transfers between devices  50.7 us (7%)
  local copies, waits for them, and re-layouts  26.9 us (4%)
  between operations  14.6 us (2%)
  other arithmetic  13.7 us (2%)
    dot_general x68, matrix products, product(): lax.dot_general(left, right, (dims, ((), ())), precision=lax.Precision.HI...  213 us
    reduce_scatter x1, waiting for transfers between devices, on_device(): lax.psum_scatter(exchange_part, 'col', scatter_dimension=0, tiled=True)  144 us
    ppermute x64, waiting for transfers between devices, exchanged(): return lax.ppermute(block, axis, route)  134 us
    reduce_scatter x7, waiting for transfers between devices, on_device(): half_x = lax.psum_scatter(partial_x, 'col', scatter_dimension=1, tiled=True)  130 us
    ppermute x64, starting transfers between devices, exchanged(): return lax.ppermute(block, axis, route)  48.9 us
  transfers between devices with their start and end apart: 72, of which 22 were waited for; matrix products, arithmetic and copies ran while one was open for 32% of the time, Pallas kernels for 0%

profile of v3, /device:TPU:0, one launch (start us, length us, event | category | flops | bytes accessed | tf_op | source)
XLA Modules:
  0.0 726.2 jit_solution(7719130844168424366)
XLA Ops:
  6.5 2.9 collective-permute-start.1
  11.0 10.6 %collective-permute-done.1 = f32[1024,128]{1,0:T(8,128)S(1)} collective-permute-done((f32[1024,128]{1,0:T(8,128)}, f32[1024,128]{1,0:T(8,128)S(1)}, u32[]{:S(2)}, u32[]{:S(2)}) %collective-permute-start.1) | collective-permute-done | bytes 524320 | tf_op jit(solution)/shard_map/ppermute | solution.py:11
  25.7 2.5 broadcast_in_dim.3
  36.6 10.9 %fusion.51 = f32[512,1024]{0,1:T(8,128)} fusion(f32[1024,1024]{1,0:T(8,128)} %constant_dynamic-update-slice_fusion.16, f32[512,12,1024]{2,0,1:T(8,128)} %param.2), kind=kOutput, calls=%fused_computation.44 | convolution fusion | flops 3221225472 | bytes 8388608 | tf_op jit(solution)/shard_map/dot_general | solution.py:15
  47.7 6.1 fusion.48
  53.9 6.2 fusion.45
  60.0 6.2 fusion.42
  66.2 3.2 pad_maximum_fusion
  69.7 6.1 fusion.63
  75.8 6.1 fusion.60
  82.0 6.2 fusion.57
  88.1 3.2 pad_maximum_fusion.1
  91.7 6.1 fusion.39
  100.1 6.5 fusion.36
  106.6 2.5 pad_maximum_fusion.2
  116.4 2.6 fusion.109
  128.9 75.5 %reduce-scatter.9.cloned.1.call-done = f32[1536,256]{1,0:T(8,128)} async-done(((f32[1536,1024]{1,0:T(8,128)}), f32[1536,256]{1,0:T(8,128)}) %reduce-scatter.9.cloned.1.call-update) | async-done | bytes 1572880 | tf_op jit(solution)/shard_map/reduce_scatter | solution.py:60
  209.1 33.3 %collective-permute-done.17 = f32[512,768]{1,0:T(8,128)S(1)} collective-permute-done((f32[512,768]{1,0:T(8,128)S(1)}, f32[512,768]{1,0:T(8,128)S(1)}, u32[]{:S(2)}, u32[]{:S(2)}) %collective-permute-start.17) | collective-permute-done | bytes 1572896 | tf_op jit(solution)/shard_map/ppermute | solution.py:11
  248.5 12.6 %collective-permute-done.21 = f32[256,768]{1,0:T(8,128)S(1)} collective-permute-done((f32[256,768]{1,0:T(8,128)S(1)}, f32[256,768]{1,0:T(8,128)S(1)}, u32[]{:S(2)}, u32[]{:S(2)}) %collective-permute-start.21) | collective-permute-done | bytes 786464 | tf_op jit(solution)/shard_map/ppermute | solution.py:11
  261.1 2.9 collective-permute-done.22
  264.1 2.5 fusion.101
  266.6 2.5 fusion.99
  271.5 2.5 fusion.97
  274.0 2.5 fusion.100
  276.5 2.5 fusion.98
  279.0 2.7 fusion.96
  281.7 36.4 %reduce-scatter.13.cloned.1.call-done = f32[1536,256]{1,0:T(8,128)} async-done(((f32[1536,1024]{1,0:T(8,128)}), f32[1536,256]{1,0:T(8,128)}) %reduce-scatter.13.cloned.1.call-update) | async-done | bytes 1572880 | tf_op jit(solution)/shard_map/reduce_scatter | solution.py:60
  323.8 10.9 %fusion.54 = f32[512,1024]{0,1:T(8,128)} fusion(f32[1024,1024]{1,0:T(8,128)} %constant_dynamic-update-slice_fusion.16, f32[512,12,1024]{2,0,1:T(8,128)} %param.2), kind=kOutput, calls=%fused_computation.45 | convolution fusion | flops 3221225472 | bytes 8388608 | tf_op jit(solution)/shard_map/dot_general | solution.py:15
  334.9 22.4 %collective-permute-done.25 = f32[512,768]{1,0:T(8,128)} collective-permute-done((f32[512,768]{1,0:T(8,128)}, f32[512,768]{1,0:T(8,128)}, u32[]{:S(2)}, u32[]{:S(2)}) %collective-permute-start.25) | collective-permute-done | bytes 1572896 | tf_op jit(solution)/shard_map/ppermute | solution.py:11
  363.6 10.9 %fusion.66 = f32[512,1024]{0,1:T(8,128)} fusion(f32[1024,1024]{1,0:T(8,128)} %constant_dynamic-update-slice_fusion.16, f32[512,12,1024]{2,0,1:T(8,128)} %param.2), kind=kOutput, calls=%fused_computation.49 | convolution fusion | flops 3221225472 | bytes 8388608 | tf_op jit(solution)/shard_map/dot_general | solution.py:15
  379.5 2.7 collective-permute-done.30
  383.4 3.9 fusion.93
  389.8 4.3 fusion.94
  394.0 2.5 fusion.89
  396.5 3.8 fusion.92
  400.3 2.5 fusion.90
  402.8 2.5 fusion.88
  410.8 21.8 %collective-permute-done.33 = f32[512,512]{1,0:T(8,128)S(1)} collective-permute-done((f32[512,512]{1,0:T(8,128)S(1)}, f32[512,512]{1,0:T(8,128)S(1)}, u32[]{:S(2)}, u32[]{:S(2)}) %collective-permute-start.33) | collective-permute-done | bytes 1048608 | tf_op jit(solution)/shard_map/ppermute | solution.py:11
  438.2 8.3 %collective-permute-done.37 = f32[256,512]{1,0:T(8,128)S(1)} collective-permute-done((f32[256,512]{1,0:T(8,128)S(1)}, f32[256,512]{1,0:T(8,128)S(1)}, u32[]{:S(2)}, u32[]{:S(2)}) %collective-permute-start.37) | collective-permute-done | bytes 524320 | tf_op jit(solution)/shard_map/ppermute | solution.py:11
  459.1 11.1 %fusion.69 = f32[512,1024]{0,1:T(8,128)} fusion(f32[1024,1024]{1,0:T(8,128)} %constant_dynamic-update-slice_fusion.16, f32[512,12,1024]{2,0,1:T(8,128)} %param.2), kind=kOutput, calls=%fused_computation.50 | convolution fusion | flops 3221225472 | bytes 8388608 | tf_op jit(solution)/shard_map/dot_general | solution.py:15
  475.3 2.7 fusion.117
  479.6 2.7 fusion.116
  492.7 2.9 fusion.123
  495.6 7.8 %collective-permute-done.49 = f32[512,256]{0,1:T(8,128)S(1)} collective-permute-done((f32[512,256]{0,1:T(8,128)}, f32[512,256]{0,1:T(8,128)S(1)}, u32[]{:S(2)}, u32[]{:S(2)}) %collective-permute-start.49) | collective-permute-done | bytes 524320 | tf_op jit(solution)/shard_map/ppermute | solution.py:11
  518.6 16.6 %reduce-scatter.21.cloned.1.call-done = f32[512,256]{0,1:T(8,128)} async-done(((f32[512,1024]{0,1:T(8,128)}), f32[512,256]{0,1:T(8,128)}) %reduce-scatter.21.cloned.1.call-update) | async-done | bytes 524304 | tf_op jit(solution)/shard_map/reduce_scatter | solution.py:60
  538.3 5.3 fusion.79
  543.6 5.5 collective-permute-done.57
  570.6 143.5 %reduce-scatter.23.cloned.1.call-done = f32[128,4096]{1,0:T(8,128)} async-done(((f32[512,4096]{1,0:T(8,128)}), f32[128,4096]{1,0:T(8,128)}) %reduce-scatter.23.cloned.1.call-update) | async-done | bytes 2097168 | tf_op jit(solution)/shard_map/reduce_scatter | solution.py:73
  (328 shorter events, 153.3 us)
Async XLA Ops:
  6.5 91.2 %reduce-scatter.11.cloned.1.call-start = ((), (), s32[]{:S(2)}) async-start(), calls=%async_computation.9 | async-start | bytes 2621440 | tf_op jit(solution)/shard_map/reduce_scatter | solution.py:60
  6.5 15.1 %collective-permute-start.1 = (f32[1024,128]{1,0:T(8,128)}, f32[1024,128]{1,0:T(8,128)S(1)}, u32[]{:S(2)}, u32[]{:S(2)}) collective-permute-start(f32[1024,128]{1,0:T(8,128)} %param.3), channel_id=1, source_target_pairs={{0,8},{4,12},{8,0},{12,4},{16,24},{20,28},{24,16},{28,20},{1,9},{5... | collective-permute-start | bytes 1572872 | tf_op jit(solution)/shard_map/ppermute | solution.py:11
  9.5 14.0 %collective-permute-start.3 = (f32[1024,128]{1,0:T(8,128)}, f32[1024,128]{1,0:T(8,128)S(1)}, u32[]{:S(2)}, u32[]{:S(2)}) collective-permute-start(f32[1024,128]{1,0:T(8,128)} %param.3), channel_id=1, source_target_pairs={{0,16},{4,20},{8,24},{12,28},{16,0},{20,4},{24,8},{28,12},{1,17},{... | collective-permute-start | bytes 1572872 | tf_op jit(solution)/shard_map/ppermute | solution.py:11
  11.0 18.6 %collective-permute-start = (f32[1024,128]{1,0:T(8,128)}, f32[1024,128]{1,0:T(8,128)S(1)}, u32[]{:S(2)}, u32[]{:S(2)}) collective-permute-start(f32[1024,128]{1,0:T(8,128)} %param.3), channel_id=1, source_target_pairs={{0,4},{4,0},{8,12},{12,8},{16,20},{20,16},{24,28},{28,24},{1,5},{5... | collective-permute-start | bytes 1572872 | tf_op jit(solution)/shard_map/ppermute | solution.py:11
  47.5 156.9 %reduce-scatter.9.cloned.1.call-start = ((), (), s32[]{:S(2)}) async-start(), calls=%async_computation.8 | async-start | bytes 7864320 | tf_op jit(solution)/shard_map/reduce_scatter | solution.py:60
  69.4 248.7 %reduce-scatter.13.cloned.1.call-start = ((), (), s32[]{:S(2)}) async-start(), calls=%async_computation.10 | async-start | bytes 7864320 | tf_op jit(solution)/shard_map/reduce_scatter | solution.py:60
  91.4 314.0 %reduce-scatter.15.cloned.1.call-start = ((), (), s32[]{:S(2)}) async-start(), calls=%async_computation.11 | async-start | bytes 5242880 | tf_op jit(solution)/shard_map/reduce_scatter | solution.py:60
  97.8 14.7 %collective-permute-start.9 = (f32[512,256]{0,1:T(8,128)}, f32[512,256]{0,1:T(8,128)}, u32[]{:S(2)}, u32[]{:S(2)}) collective-permute-start(f32[512,256]{0,1:T(8,128)} %reduce-scatter.11.cloned.1.call-done), channel_id=1, source_target_pairs={{0,8},{4,12},{8,0},{12,4},{16,24},{20,28},{24,16},{28,20},{1,9},{5... | collective-permute-start | bytes 1572872 | tf_op jit(solution)/shard_map/ppermute | solution.py:11
  99.5 15.3 %collective-permute-start.11 = (f32[512,256]{0,1:T(8,128)}, f32[512,256]{0,1:T(8,128)S(1)}, u32[]{:S(2)}, u32[]{:S(2)}) collective-permute-start(f32[512,256]{0,1:T(8,128)} %reduce-scatter.11.cloned.1.call-done), channel_id=1, source_target_pairs={{0,16},{4,20},{8,24},{12,28},{16,0},{20,4},{24,8},{28,12},{1,17},{... | collective-permute-start | bytes 1572872 | tf_op jit(solution)/shard_map/ppermute | solution.py:11
  109.1 11.5 %collective-permute-start.8 = (f32[512,256]{0,1:T(8,128)S(1)}, f32[512,256]{0,1:T(8,128)S(1)}, u32[]{:S(2)}, u32[]{:S(2)}) collective-permute-start(f32[512,256]{0,1:T(8,128)S(1)} %copy-done.3), channel_id=1, source_target_pairs={{0,4},{4,0},{8,12},{12,8},{16,20},{20,16},{24,28},{28,24},{1,5},{5... | collective-permute-start | bytes 1572872 | tf_op jit(solution)/shard_map/ppermute | solution.py:11
  204.5 252.2 %reduce-scatter.17.cloned.1.call-start = ((), (), s32[]{:S(2)}) async-start(), calls=%async_computation.12 | async-start | bytes 2621440 | tf_op jit(solution)/shard_map/reduce_scatter | solution.py:60
  206.1 36.3 %collective-permute-start.17 = (f32[512,768]{1,0:T(8,128)S(1)}, f32[512,768]{1,0:T(8,128)S(1)}, u32[]{:S(2)}, u32[]{:S(2)}) collective-permute-start(f32[512,768]{1,0:T(8,128)S(1)} %pad_maximum_fusion.3), channel_id=1, source_target_pairs={{0,8},{4,12},{8,0},{12,4},{16,24},{20,28},{24,16},{28,20},{1,9},{5... | collective-permute-start | bytes 4718600 | tf_op jit(solution)/shard_map/ppermute | solution.py:11
  207.6 36.3 %collective-permute-start.19 = (f32[512,768]{1,0:T(8,128)S(1)}, f32[512,768]{1,0:T(8,128)S(1)}, u32[]{:S(2)}, u32[]{:S(2)}) collective-permute-start(f32[512,768]{1,0:T(8,128)S(1)} %pad_maximum_fusion.3), channel_id=1, source_target_pairs={{0,16},{4,20},{8,24},{12,28},{16,0},{20,4},{24,8},{28,12},{1,17},{... | collective-permute-start | bytes 4718600 | tf_op jit(solution)/shard_map/ppermute | solution.py:11
  242.4 18.7 %collective-permute-start.21 = (f32[256,768]{1,0:T(8,128)S(1)}, f32[256,768]{1,0:T(8,128)S(1)}, u32[]{:S(2)}, u32[]{:S(2)}) collective-permute-start(f32[256,768]{1,0:T(8,128)S(1)} %slice.159), channel_id=1, source_target_pairs={{0,16},{4,20},{8,24},{12,28},{16,0},{20,4},{24,8},{28,12},{1,17},{... | collective-permute-start | bytes 2359304 | tf_op jit(solution)/shard_map/ppermute | solution.py:11
  243.9 25.2 %collective-permute-start.16 = (f32[512,768]{1,0:T(8,128)S(1)}, f32[512,768]{1,0:T(8,128)S(1)}, u32[]{:S(2)}, u32[]{:S(2)}) collective-permute-start(f32[512,768]{1,0:T(8,128)S(1)} %pad_maximum_fusion.3), channel_id=1, source_target_pairs={{0,4},{4,0},{8,12},{12,8},{16,20},{20,16},{24,28},{28,24},{1,5},{5... | collective-permute-start | bytes 4718600 | tf_op jit(solution)/shard_map/ppermute | solution.py:11
  244.0 20.0 %collective-permute-start.22 = (f32[256,768]{1,0:T(8,128)S(1)}, f32[256,768]{1,0:T(8,128)S(1)}, u32[]{:S(2)}, u32[]{:S(2)}) collective-permute-start(f32[256,768]{1,0:T(8,128)S(1)} %slice.160), channel_id=1, source_target_pairs={{0,8},{4,12},{8,0},{12,4},{16,24},{20,28},{24,16},{28,20},{1,9},{5... | collective-permute-start | bytes 2359304 | tf_op jit(solution)/shard_map/ppermute | solution.py:11
  245.5 28.5 %collective-permute-start.18 = (f32[512,768]{1,0:T(8,128)S(1)}, f32[512,768]{1,0:T(8,128)S(1)}, u32[]{:S(2)}, u32[]{:S(2)}) collective-permute-start(f32[512,768]{1,0:T(8,128)S(1)} %collective-permute-done.17), channel_id=1, source_target_pairs={{0,4},{4,0},{8,12},{12,8},{16,20},{20,16},{24,28},{28,24},{1,5},{5... | collective-permute-start | bytes 4718600 | tf_op jit(solution)/shard_map/ppermute | solution.py:11
  248.2 28.3 %collective-permute-start.20 = (f32[512,768]{1,0:T(8,128)S(1)}, f32[512,768]{1,0:T(8,128)S(1)}, u32[]{:S(2)}, u32[]{:S(2)}) collective-permute-start(f32[512,768]{1,0:T(8,128)S(1)} %collective-permute-done.19), channel_id=1, source_target_pairs={{0,4},{4,0},{8,12},{12,8},{16,20},{20,16},{24,28},{28,24},{1,5},{5... | collective-permute-start | bytes 4718600 | tf_op jit(solution)/shard_map/ppermute | solution.py:11
  264.1 15.0 %collective-permute-start.23 = (f32[512,768]{1,0:T(8,128)S(1)}, f32[512,768]{1,0:T(8,128)S(1)}, u32[]{:S(2)}, u32[]{:S(2)}) collective-permute-start(f32[512,768]{1,0:T(8,128)S(1)} %constant_dynamic-update-slice_fusion.4), channel_id=1, source_target_pairs={{0,4},{4,0},{8,12},{12,8},{16,20},{20,16},{24,28},{28,24},{1,5},{5... | collective-permute-start | bytes 4718600 | tf_op jit(solution)/shard_map/ppermute | solution.py:11
  320.9 36.5 %collective-permute-start.25 = (f32[512,768]{1,0:T(8,128)}, f32[512,768]{1,0:T(8,128)}, u32[]{:S(2)}, u32[]{:S(2)}) collective-permute-start(f32[512,768]{1,0:T(8,128)} %pad_maximum_fusion.4), channel_id=1, source_target_pairs={{0,8},{4,12},{8,0},{12,4},{16,24},{20,28},{24,16},{28,20},{1,9},{5... | collective-permute-start | bytes 4718600 | tf_op jit(solution)/shard_map/ppermute | solution.py:11
  322.3 38.6 %collective-permute-start.27 = (f32[512,768]{1,0:T(8,128)}, f32[512,768]{1,0:T(8,128)S(1)}, u32[]{:S(2)}, u32[]{:S(2)}) collective-permute-start(f32[512,768]{1,0:T(8,128)} %pad_maximum_fusion.4), channel_id=1, source_target_pairs={{0,16},{4,20},{8,24},{12,28},{16,0},{20,4},{24,8},{28,12},{1,17},{... | collective-permute-start | bytes 4718600 | tf_op jit(solution)/shard_map/ppermute | solution.py:11
  334.7 155.0 %reduce-scatter.19.cloned.1.call-start = ((), (), s32[]{:S(2)}) async-start(), calls=%async_computation.13 | async-start | bytes 2621440 | tf_op jit(solution)/shard_map/reduce_scatter | solution.py:60
  359.5 18.8 %collective-permute-start.29 = (f32[256,768]{1,0:T(8,128)}, f32[256,768]{1,0:T(8,128)}, u32[]{:S(2)}, u32[]{:S(2)}) collective-permute-start(f32[256,768]{1,0:T(8,128)} %slice.161), channel_id=1, source_target_pairs={{0,16},{4,20},{8,24},{12,28},{16,0},{20,4},{24,8},{28,12},{1,17},{... | collective-permute-start | bytes 2359304 | tf_op jit(solution)/shard_map/ppermute | solution.py:11
  361.0 28.8 %collective-permute-start.24 = (f32[512,768]{1,0:T(8,128)}, f32[512,768]{1,0:T(8,128)}, u32[]{:S(2)}, u32[]{:S(2)}) collective-permute-start(f32[512,768]{1,0:T(8,128)} %pad_maximum_fusion.4), channel_id=1, source_target_pairs={{0,4},{4,0},{8,12},{12,8},{16,20},{20,16},{24,28},{28,24},{1,5},{5... | collective-permute-start | bytes 4718600 | tf_op jit(solution)/shard_map/ppermute | solution.py:11
  361.9 20.3 %collective-permute-start.30 = (f32[256,768]{1,0:T(8,128)}, f32[256,768]{1,0:T(8,128)}, u32[]{:S(2)}, u32[]{:S(2)}) collective-permute-start(f32[256,768]{1,0:T(8,128)} %slice.162), channel_id=1, source_target_pairs={{0,8},{4,12},{8,0},{12,4},{16,24},{20,28},{24,16},{28,20},{1,9},{5... | collective-permute-start | bytes 2359304 | tf_op jit(solution)/shard_map/ppermute | solution.py:11
  363.4 33.1 %collective-permute-start.26 = (f32[512,768]{1,0:T(8,128)}, f32[512,768]{1,0:T(8,128)}, u32[]{:S(2)}, u32[]{:S(2)}) collective-permute-start(f32[512,768]{1,0:T(8,128)} %collective-permute-done.25), channel_id=1, source_target_pairs={{0,4},{4,0},{8,12},{12,8},{16,20},{20,16},{24,28},{28,24},{1,5},{5... | collective-permute-start | bytes 4718600 | tf_op jit(solution)/shard_map/ppermute | solution.py:11
  376.9 23.4 %collective-permute-start.28 = (f32[512,768]{1,0:T(8,128)S(1)}, f32[512,768]{1,0:T(8,128)S(1)}, u32[]{:S(2)}, u32[]{:S(2)}) collective-permute-start(f32[512,768]{1,0:T(8,128)S(1)} %collective-permute-done.27), channel_id=1, source_target_pairs={{0,4},{4,0},{8,12},{12,8},{16,20},{20,16},{24,28},{28,24},{1,5},{5... | collective-permute-start | bytes 4718600 | tf_op jit(solution)/shard_map/ppermute | solution.py:11
  383.4 19.4 %collective-permute-start.31 = (f32[512,768]{1,0:T(8,128)S(1)}, f32[512,768]{1,0:T(8,128)S(1)}, u32[]{:S(2)}, u32[]{:S(2)}) collective-permute-start(f32[512,768]{1,0:T(8,128)S(1)} %constant_dynamic-update-slice_fusion.6), channel_id=1, source_target_pairs={{0,4},{4,0},{8,12},{12,8},{16,20},{20,16},{24,28},{28,24},{1,5},{5... | collective-permute-start | bytes 4718600 | tf_op jit(solution)/shard_map/ppermute | solution.py:11
  405.4 129.9 %reduce-scatter.21.cloned.1.call-start = ((), (), s32[]{:S(2)}) async-start(), calls=%async_computation.14 | async-start | bytes 2621440 | tf_op jit(solution)/shard_map/reduce_scatter | solution.py:60
  406.9 25.7 %collective-permute-start.33 = (f32[512,512]{1,0:T(8,128)S(1)}, f32[512,512]{1,0:T(8,128)S(1)}, u32[]{:S(2)}, u32[]{:S(2)}) collective-permute-start(f32[512,512]{1,0:T(8,128)S(1)} %pad_maximum_fusion.5), channel_id=1, source_target_pairs={{0,8},{4,12},{8,0},{12,4},{16,24},{20,28},{24,16},{28,20},{1,9},{5... | collective-permute-start | bytes 3145736 | tf_op jit(solution)/shard_map/ppermute | solution.py:11
  408.3 25.4 %collective-permute-start.35 = (f32[512,512]{1,0:T(8,128)S(1)}, f32[512,512]{1,0:T(8,128)S(1)}, u32[]{:S(2)}, u32[]{:S(2)}) collective-permute-start(f32[512,512]{1,0:T(8,128)S(1)} %pad_maximum_fusion.5), channel_id=1, source_target_pairs={{0,16},{4,20},{8,24},{12,28},{16,0},{20,4},{24,8},{28,12},{1,17},{... | collective-permute-start | bytes 3145736 | tf_op jit(solution)/shard_map/ppermute | solution.py:11
  408.8 38.6 %collective-permute-start.32 = (f32[512,512]{1,0:T(8,128)S(1)}, f32[512,512]{1,0:T(8,128)S(1)}, u32[]{:S(2)}, u32[]{:S(2)}) collective-permute-start(f32[512,512]{1,0:T(8,128)S(1)} %pad_maximum_fusion.5), channel_id=1, source_target_pairs={{0,4},{4,0},{8,12},{12,8},{16,20},{20,16},{24,28},{28,24},{1,5},{5... | collective-permute-start | bytes 3145736 | tf_op jit(solution)/shard_map/ppermute | solution.py:11
  432.7 13.8 %collective-permute-start.37 = (f32[256,512]{1,0:T(8,128)S(1)}, f32[256,512]{1,0:T(8,128)S(1)}, u32[]{:S(2)}, u32[]{:S(2)}) collective-permute-start(f32[256,512]{1,0:T(8,128)S(1)} %slice.163), channel_id=1, source_target_pairs={{0,16},{4,20},{8,24},{12,28},{16,0},{20,4},{24,8},{28,12},{1,17},{... | collective-permute-start | bytes 1572872 | tf_op jit(solution)/shard_map/ppermute | solution.py:11
  433.8 13.6 %collective-permute-start.38 = (f32[256,512]{1,0:T(8,128)S(1)}, f32[256,512]{1,0:T(8,128)S(1)}, u32[]{:S(2)}, u32[]{:S(2)}) collective-permute-start(f32[256,512]{1,0:T(8,128)S(1)} %slice.164), channel_id=1, source_target_pairs={{0,8},{4,12},{8,0},{12,4},{16,24},{20,28},{24,16},{28,20},{1,9},{5... | collective-permute-start | bytes 1572872 | tf_op jit(solution)/shard_map/ppermute | solution.py:11
  436.6 13.9 %collective-permute-start.34 = (f32[512,512]{1,0:T(8,128)S(1)}, f32[512,512]{1,0:T(8,128)S(1)}, u32[]{:S(2)}, u32[]{:S(2)}) collective-permute-start(f32[512,512]{1,0:T(8,128)S(1)} %collective-permute-done.33), channel_id=1, source_target_pairs={{0,4},{4,0},{8,12},{12,8},{16,20},{20,16},{24,28},{28,24},{1,5},{5... | collective-permute-start | bytes 3145736 | tf_op jit(solution)/shard_map/ppermute | solution.py:11
  436.6 16.0 %collective-permute-start.36 = (f32[512,512]{1,0:T(8,128)S(1)}, f32[512,512]{1,0:T(8,128)S(1)}, u32[]{:S(2)}, u32[]{:S(2)}) collective-permute-start(f32[512,512]{1,0:T(8,128)S(1)} %collective-permute-done.35), channel_id=1, source_target_pairs={{0,4},{4,0},{8,12},{12,8},{16,20},{20,16},{24,28},{28,24},{1,5},{5... | collective-permute-start | bytes 3145736 | tf_op jit(solution)/shard_map/ppermute | solution.py:11
  456.7 15.1 %collective-permute-start.41 = (f32[512,256]{0,1:T(8,128)}, f32[512,256]{0,1:T(8,128)}, u32[]{:S(2)}, u32[]{:S(2)}) collective-permute-start(f32[512,256]{0,1:T(8,128)} %reduce-scatter.17.cloned.1.call-done), channel_id=1, source_target_pairs={{0,8},{4,12},{8,0},{12,4},{16,24},{20,28},{24,16},{28,20},{1,9},{5... | collective-permute-start | bytes 1572872 | tf_op jit(solution)/shard_map/ppermute | solution.py:11
  457.3 16.0 %collective-permute-start.43 = (f32[512,256]{0,1:T(8,128)}, f32[512,256]{0,1:T(8,128)S(1)}, u32[]{:S(2)}, u32[]{:S(2)}) collective-permute-start(f32[512,256]{0,1:T(8,128)} %reduce-scatter.17.cloned.1.call-done), channel_id=1, source_target_pairs={{0,16},{4,20},{8,24},{12,28},{16,0},{20,4},{24,8},{28,12},{1,17},{... | collective-permute-start | bytes 1572872 | tf_op jit(solution)/shard_map/ppermute | solution.py:11
  470.2 244.0 %reduce-scatter.23.cloned.1.call-start = ((), (), s32[]{:S(2)}) async-start(), calls=%async_computation.15 | async-start | bytes 10485760 | tf_op jit(solution)/shard_map/reduce_scatter | solution.py:73
  474.8 10.8 %collective-permute-start.44 = (f32[512,256]{0,1:T(8,128)S(1)}, f32[512,256]{0,1:T(8,128)S(1)}, u32[]{:S(2)}, u32[]{:S(2)}) collective-permute-start(f32[512,256]{0,1:T(8,128)S(1)} %collective-permute-done.43), channel_id=1, source_target_pairs={{0,4},{4,0},{8,12},{12,8},{16,20},{20,16},{24,28},{28,24},{1,5},{5... | collective-permute-start | bytes 1572872 | tf_op jit(solution)/shard_map/ppermute | solution.py:11
  489.7 13.7 %collective-permute-start.49 = (f32[512,256]{0,1:T(8,128)}, f32[512,256]{0,1:T(8,128)S(1)}, u32[]{:S(2)}, u32[]{:S(2)}) collective-permute-start(f32[512,256]{0,1:T(8,128)} %reduce-scatter.19.cloned.1.call-done), channel_id=1, source_target_pairs={{0,8},{4,12},{8,0},{12,4},{16,24},{20,28},{24,16},{28,20},{1,9},{5... | collective-permute-start | bytes 1572872 | tf_op jit(solution)/shard_map/ppermute | solution.py:11
  491.2 13.8 %collective-permute-start.51 = (f32[512,256]{0,1:T(8,128)}, f32[512,256]{0,1:T(8,128)S(1)}, u32[]{:S(2)}, u32[]{:S(2)}) collective-permute-start(f32[512,256]{0,1:T(8,128)} %reduce-scatter.19.cloned.1.call-done), channel_id=1, source_target_pairs={{0,16},{4,20},{8,24},{12,28},{16,0},{20,4},{24,8},{28,12},{1,17},{... | collective-permute-start | bytes 1572872 | tf_op jit(solution)/shard_map/ppermute | solution.py:11
  492.7 17.7 %collective-permute-start.48 = (f32[512,256]{0,1:T(8,128)}, f32[512,256]{0,1:T(8,128)S(1)}, u32[]{:S(2)}, u32[]{:S(2)}) collective-permute-start(f32[512,256]{0,1:T(8,128)} %reduce-scatter.19.cloned.1.call-done), channel_id=1, source_target_pairs={{0,4},{4,0},{8,12},{12,8},{16,20},{20,16},{24,28},{28,24},{1,5},{5... | collective-permute-start | bytes 1572872 | tf_op jit(solution)/shard_map/ppermute | solution.py:11
  535.3 13.8 %collective-permute-start.57 = (f32[512,256]{0,1:T(8,128)}, f32[512,256]{0,1:T(8,128)S(1)}, u32[]{:S(2)}, u32[]{:S(2)}) collective-permute-start(f32[512,256]{0,1:T(8,128)} %reduce-scatter.21.cloned.1.call-done), channel_id=1, source_target_pairs={{0,8},{4,12},{8,0},{12,4},{16,24},{20,28},{24,16},{28,20},{1,9},{5... | collective-permute-start | bytes 1572872 | tf_op jit(solution)/shard_map/ppermute | solution.py:11
  536.8 13.8 %collective-permute-start.59 = (f32[512,256]{0,1:T(8,128)}, f32[512,256]{0,1:T(8,128)S(1)}, u32[]{:S(2)}, u32[]{:S(2)}) collective-permute-start(f32[512,256]{0,1:T(8,128)} %reduce-scatter.21.cloned.1.call-done), channel_id=1, source_target_pairs={{0,16},{4,20},{8,24},{12,28},{16,0},{20,4},{24,8},{28,12},{1,17},{... | collective-permute-start | bytes 1572872 | tf_op jit(solution)/shard_map/ppermute | solution.py:11
  538.3 14.5 %collective-permute-start.56 = (f32[512,256]{0,1:T(8,128)}, f32[512,256]{0,1:T(8,128)S(1)}, u32[]{:S(2)}, u32[]{:S(2)}) collective-permute-start(f32[512,256]{0,1:T(8,128)} %reduce-scatter.21.cloned.1.call-done), channel_id=1, source_target_pairs={{0,4},{4,0},{8,12},{12,8},{16,20},{20,16},{24,28},{28,24},{1,5},{5... | collective-permute-start | bytes 1572872 | tf_op jit(solution)/shard_map/ppermute | solution.py:11
  552.2 10.1 %collective-permute-start.60 = (f32[512,256]{0,1:T(8,128)S(1)}, f32[512,256]{0,1:T(8,128)S(1)}, u32[]{:S(2)}, u32[]{:S(2)}) collective-permute-start(f32[512,256]{0,1:T(8,128)S(1)} %collective-permute-done.59), channel_id=1, source_target_pairs={{0,4},{4,0},{8,12},{12,8},{16,20},{20,16},{24,28},{28,24},{1,5},{5... | collective-permute-start | bytes 1572872 | tf_op jit(solution)/shard_map/ppermute | solution.py:11
  557.5 9.9 %collective-permute-start.63 = (f32[512,256]{0,1:T(8,128)S(1)}, f32[512,256]{0,1:T(8,128)S(1)}, u32[]{:S(2)}, u32[]{:S(2)}) collective-permute-start(f32[512,256]{0,1:T(8,128)S(1)} %constant_dynamic-update-slice_fusion.14), channel_id=1, source_target_pairs={{0,4},{4,0},{8,12},{12,8},{16,20},{20,16},{24,28},{28,24},{1,5},{5... | collective-permute-start | bytes 1572872 | tf_op jit(solution)/shard_map/ppermute | solution.py:11
  (73 other events, 442.7 us)
Sparse Core Ops, SparseCore 0:
  47.6 44.2 reduce-scatter.10
  94.3 110.0 reduce-scatter.8
  206.9 111.2 reduce-scatter.12
  320.4 77.2 reduce-scatter.14
  399.9 44.3 reduce-scatter.16
  446.5 43.1 reduce-scatter.18
  492.0 43.1 reduce-scatter.20
  570.7 143.3 reduce-scatter.22

commit v4 on v3

--- a/solution.py
+++ b/solution.py
@@ -38,6 +38,55 @@
     return [held[j] for j in range(count)]
 
 
+def in_order(parts, index):
+    flip = 1
+    while flip < len(parts):
+        swap = (index & flip) != 0
+        parts = [jnp.where(swap, parts[j ^ flip], parts[j]) for j in range(len(parts))]
+        flip *= 2
+    return parts
+
+
+def side(index, j):
+    return (index >> (j.bit_length() - 1)) & 1
+
+
+def gram_tiles(own, blocks, place):
+    half = own.shape[0] // 2
+    tiles = [product(own, own, ((1,), (1,)))]
+    for j in range(1, len(blocks)):
+        for r in range(2):
+            start = (side(place, j) ^ r) * half
+            other = lax.dynamic_slice_in_dim(blocks[j], start, half, axis=0)
+            tiles.append(product(own[r * half : (r + 1) * half], other, ((1,), (1,))))
+    return tiles
+
+
+def mirrored(rows, row_count, place):
+    blk_size, col_size = lax.axis_size("blk"), lax.axis_size("col")
+    half, share, pieces = row_count // 2, row_count // col_size, col_size // 2
+    col = lax.axis_index("col")
+    high, low = col // pieces, col % pieces
+    flipped = rows[:, row_count:].T
+    blocks = [rows[:, :row_count]]
+    for j in range(1, blk_size):
+        got = []
+        for t in range(pieces):
+            route = []
+            for b in range(blk_size):
+                for c in range(col_size):
+                    target = ((c // pieces) ^ side(b, j)) * pieces + ((c % pieces) ^ t)
+                    route.append((b * col_size + c, (b ^ j) * col_size + target))
+            piece = lax.dynamic_slice_in_dim(
+                flipped, (j - 1) * half + (low ^ t) * share, share, axis=0
+            )
+            got.append(lax.ppermute(piece, ("blk", "col"), route))
+        other = jnp.concatenate(in_order(got, low), axis=1)
+        mine = rows[:, row_count + (j - 1) * half : row_count + j * half]
+        blocks.append(jnp.concatenate(in_order([mine, other], high ^ side(place, j)), axis=1))
+    return jnp.concatenate(in_order(blocks, place), axis=1)
+
+
 def on_device(three_index, coefficients):
     row_count, aux_count, _ = three_index.shape
     blk_size = lax.axis_size("blk")
@@ -66,18 +115,15 @@
             [half_x[p * row_count : (p + 1) * row_count] for p in range(per_group)], axis=1
         )
         blocks = blocks_of_others(own, "blk")
-        earlier.append([product(own, block, ((1,), (1,))) for block in blocks])
+        earlier.append(gram_tiles(own, blocks, place))
     for terms in earlier[-3:]:
         tiles = [t + u for t, u in zip(tiles, terms)]
-    exchange_part = jnp.concatenate(tiles, axis=1)
+    stacked = [
+        jnp.concatenate(tiles[2 * j - 1 : 2 * j + 1], axis=0) for j in range(1, blk_size)
+    ]
+    exchange_part = jnp.concatenate([tiles[0]] + stacked, axis=1)
     rows = lax.psum_scatter(exchange_part, "col", scatter_dimension=0, tiled=True)
-    shares = jnp.split(rows, blk_size, axis=1)
-    flip = 1
-    while flip < blk_size:
-        swap = (place & flip) != 0
-        shares = [jnp.where(swap, shares[j ^ flip], shares[j]) for j in range(blk_size)]
-        flip *= 2
-    return jnp.concatenate(shares, axis=1)
+    return mirrored(rows, row_count, place)
 
 
 def solution(mesh):

time: 733 us -> 710 us (0.969)
  waiting for transfers between devices: 407 us -> 326 us
  starting transfers between devices: 50.7 us -> 81.9 us
  matrix products: 213 us -> 232 us
    reduce_scatter x1, waiting for transfers between devices: 144 us -> 83.7 us  [on_device(): lax.psum_scatter(exchange_part, 'col', scatter_dimension=0, tiled=True)]
    ppermute x64, waiting for transfers between devices: 134 us -> 100 us  [exchanged(): return lax.ppermute(block, axis, route)]
    ppermute x0 -> x14, starting transfers between devices: none -> 28 us  [mirrored(): got.append(lax.ppermute(piece, ('blk', 'col'), route))]
    dot_general x68 -> x117, matrix products: 213 us -> 232 us  [product(): lax.dot_general(left, right, (dims, ((), ())), precision=lax.Precision.HI...]
    ppermute x0 -> x14, waiting for transfers between devices: none -> 8.91 us  [mirrored(): got.append(lax.ppermute(piece, ('blk', 'col'), route))]
  transfers between devices with their start and end apart: 72 -> 86, of which waited for: 22 -> 21; matrix products, arithmetic and copies ran while one was open for 32% -> 36% of each run, Pallas kernels for 0% -> 0%
where the time goes in v4:
time: 710 us; the launch traced here: 701 us
  waiting for transfers between devices  326 us (46%)
  matrix products  232 us (33%)
  starting transfers between devices  81.9 us (12%)
  local copies, waits for them, and re-layouts  26.9 us (4%)
  other arithmetic  18.5 us (3%)
  between operations  15.7 us (2%)
    dot_general x117, matrix products, product(): lax.dot_general(left, right, (dims, ((), ())), precision=lax.Precision.HI...  232 us
    reduce_scatter x7, waiting for transfers between devices, on_device(): half_x = lax.psum_scatter(partial_x, 'col', scatter_dimension=1, tiled=True)  133 us
    ppermute x64, waiting for transfers between devices, exchanged(): return lax.ppermute(block, axis, route)  100 us
    reduce_scatter x1, waiting for transfers between devices, on_device(): lax.psum_scatter(exchange_part, 'col', scatter_dimension=0, tiled=True)  83.7 us
    ppermute x64, starting transfers between devices, exchanged(): return lax.ppermute(block, axis, route)  52.6 us
    ppermute x14, starting transfers between devices, mirrored(): got.append(lax.ppermute(piece, ('blk', 'col'), route))  28 us
  transfers between devices with their start and end apart: 86, of which 21 were waited for; matrix products, arithmetic and copies ran while one was open for 36% of the time, Pallas kernels for 0%

profile of v4, /device:TPU:0, one launch (start us, length us, event | category | flops | bytes accessed | tf_op | source)
XLA Modules:
  0.0 701.2 jit_solution(11578803136615602138)
XLA Ops:
  6.5 2.9 collective-permute-start.1
  11.0 10.6 %collective-permute-done.1 = f32[1024,128]{1,0:T(8,128)S(1)} collective-permute-done((f32[1024,128]{1,0:T(8,128)}, f32[1024,128]{1,0:T(8,128)S(1)}, u32[]{:S(2)}, u32[]{:S(2)}) %collective-permute-start.1) | collective-permute-done | bytes 524320 | tf_op jit(solution)/shard_map/ppermute | solution.py:11
  25.7 2.6 broadcast_in_dim.3
  36.6 10.9 %fusion.51 = f32[512,1024]{0,1:T(8,128)} fusion(f32[1024,1024]{1,0:T(8,128)} %constant_dynamic-update-slice_fusion.16, f32[512,12,1024]{2,0,1:T(8,128)} %param.2), kind=kOutput, calls=%fused_computation.44 | convolution fusion | flops 3221225472 | bytes 8388608 | tf_op jit(solution)/shard_map/dot_general | solution.py:15
  47.7 6.1 fusion.48
  53.8 6.2 fusion.45
  60.0 6.2 fusion.42
  66.2 3.3 pad_maximum_fusion
  69.8 6.1 fusion.63
  75.9 6.1 fusion.60
  82.0 6.2 fusion.57
  88.2 3.3 pad_maximum_fusion.1
  92.0 6.1 fusion.39
  100.9 6.2 fusion.36
  107.1 2.5 pad_maximum_fusion.2
  110.3 2.5 collective-permute-done.9
  136.2 68.2 %reduce-scatter.9.cloned.1.call-done = f32[1536,256]{1,0:T(8,128)} async-done(((f32[1536,1024]{1,0:T(8,128)}), f32[1536,256]{1,0:T(8,128)}) %reduce-scatter.9.cloned.1.call-update) | async-done | bytes 1572880 | tf_op jit(solution)/shard_map/reduce_scatter | solution.py:109
  209.1 2.5 fusion.447
  211.5 30.8 %collective-permute-done.17 = f32[512,768]{1,0:T(8,128)S(1)} collective-permute-done((f32[512,768]{1,0:T(8,128)S(1)}, f32[512,768]{1,0:T(8,128)S(1)}, u32[]{:S(2)}, u32[]{:S(2)}) %collective-permute-start.17) | collective-permute-done | bytes 1572896 | tf_op jit(solution)/shard_map/ppermute | solution.py:11
  252.5 8.5 %collective-permute-done.21 = f32[256,768]{1,0:T(8,128)S(1)} collective-permute-done((f32[256,768]{1,0:T(8,128)S(1)}, f32[256,768]{1,0:T(8,128)S(1)}, u32[]{:S(2)}, u32[]{:S(2)}) %collective-permute-start.21) | collective-permute-done | bytes 786464 | tf_op jit(solution)/shard_map/ppermute | solution.py:11
  274.0 44.2 %reduce-scatter.13.cloned.1.call-done = f32[1536,256]{1,0:T(8,128)} async-done(((f32[1536,1024]{1,0:T(8,128)}), f32[1536,256]{1,0:T(8,128)}) %reduce-scatter.13.cloned.1.call-update) | async-done | bytes 1572880 | tf_op jit(solution)/shard_map/reduce_scatter | solution.py:109
  322.8 11.3 %fusion.54 = f32[512,1024]{0,1:T(8,128)} fusion(f32[1024,1024]{1,0:T(8,128)} %constant_dynamic-update-slice_fusion.16, f32[512,12,1024]{2,0,1:T(8,128)} %param.2), kind=kOutput, calls=%fused_computation.45 | convolution fusion | flops 3221225472 | bytes 8388608 | tf_op jit(solution)/shard_map/dot_general | solution.py:15
  334.1 4.0 fusion.446
  338.2 18.0 %collective-permute-done.25 = f32[512,768]{1,0:T(8,128)} collective-permute-done((f32[512,768]{1,0:T(8,128)S(1)}, f32[512,768]{1,0:T(8,128)}, u32[]{:S(2)}, u32[]{:S(2)}) %collective-permute-start.25) | collective-permute-done | bytes 1572896 | tf_op jit(solution)/shard_map/ppermute | solution.py:11
  361.6 2.4 fusion.99
  364.0 2.4 fusion.97
  366.4 2.4 fusion.95
  369.3 2.4 fusion.93
  371.7 2.4 fusion.87
  376.0 2.4 collective-permute-done.30
  378.5 2.4 fusion.85
  391.1 6.7 reduce-scatter.15.cloned.1.call-done
  403.1 11.1 %fusion.66 = f32[512,1024]{0,1:T(8,128)} fusion(f32[1024,1024]{1,0:T(8,128)} %constant_dynamic-update-slice_fusion.16, f32[512,12,1024]{2,0,1:T(8,128)} %param.2), kind=kOutput, calls=%fused_computation.49 | convolution fusion | flops 3221225472 | bytes 8388608 | tf_op jit(solution)/shard_map/dot_general | solution.py:15
  416.4 9.0 %collective-permute-done.33 = f32[512,512]{1,0:T(8,128)} collective-permute-done((f32[512,512]{1,0:T(8,128)}, f32[512,512]{1,0:T(8,128)}, u32[]{:S(2)}, u32[]{:S(2)}) %collective-permute-start.33) | collective-permute-done | bytes 1048608 | tf_op jit(solution)/shard_map/ppermute | solution.py:11
  453.0 11.3 %fusion.69 = f32[512,1024]{0,1:T(8,128)} fusion(f32[1024,1024]{1,0:T(8,128)} %constant_dynamic-update-slice_fusion.16, f32[512,12,1024]{2,0,1:T(8,128)} %param.2), kind=kOutput, calls=%fused_computation.50 | convolution fusion | flops 3221225472 | bytes 8388608 | tf_op jit(solution)/shard_map/dot_general | solution.py:15
  492.7 2.8 fusion.459
  495.5 8.0 %collective-permute-done.49 = f32[512,256]{0,1:T(8,128)S(1)} collective-permute-done((f32[512,256]{0,1:T(8,128)}, f32[512,256]{0,1:T(8,128)S(1)}, u32[]{:S(2)}, u32[]{:S(2)}) %collective-permute-start.49) | collective-permute-done | bytes 524320 | tf_op jit(solution)/shard_map/ppermute | solution.py:11
  522.9 12.3 %reduce-scatter.21.cloned.1.call-done = f32[512,256]{0,1:T(8,128)} async-done(((f32[512,1024]{0,1:T(8,128)}), f32[512,256]{0,1:T(8,128)}) %reduce-scatter.21.cloned.1.call-update) | async-done | bytes 524304 | tf_op jit(solution)/shard_map/reduce_scatter | solution.py:109
  538.3 4.3 fusion.72
  542.6 6.4 collective-permute-done.57
  567.5 83.7 %reduce-scatter.23.cloned.1.call-done = f32[128,2304]{1,0:T(8,128)} async-done(((f32[512,2304]{1,0:T(8,128)}), f32[128,2304]{1,0:T(8,128)}) %reduce-scatter.23.cloned.1.call-update) | async-done | bytes 1179664 | tf_op jit(solution)/shard_map/reduce_scatter | solution.py:125
  652.6 2.8 collective-permute-start.64
  659.2 2.4 collective-permute-start.66
  662.6 2.6 collective-permute-start.67
  665.2 4.5 collective-permute-start.75
  673.2 7.3 %collective-permute-start.73 = (f32[128,128]{1,0:T(8,128)S(1)}, f32[128,128]{1,0:T(8,128)S(1)}, u32[]{:S(2)}, u32[]{:S(2)}) collective-permute-start(f32[128,128]{1,0:T(8,128)S(1)} %bitcast.134), channel_id=1, source_target_pairs={{0,12},{1,13},{2,14},{3,15},{4,8},{5,9},{6,10},{7,11},{8,6},{9,7},... | collective-permute-start | bytes 196616 | tf_op jit(solution)/shard_map/ppermute | solution.py:83
  682.5 5.1 collective-permute-done.70
  687.7 3.3 collective-permute-done.71
  (527 shorter events, 210.0 us)
Async XLA Ops:
  6.5 91.5 %reduce-scatter.11.cloned.1.call-start = ((), (), s32[]{:S(2)}) async-start(), calls=%async_computation.9 | async-start | bytes 2621440 | tf_op jit(solution)/shard_map/reduce_scatter | solution.py:109
  6.5 15.1 %collective-permute-start.1 = (f32[1024,128]{1,0:T(8,128)}, f32[1024,128]{1,0:T(8,128)S(1)}, u32[]{:S(2)}, u32[]{:S(2)}) collective-permute-start(f32[1024,128]{1,0:T(8,128)} %param.3), channel_id=1, source_target_pairs={{0,8},{4,12},{8,0},{12,4},{16,24},{20,28},{24,16},{28,20},{1,9},{5... | collective-permute-start | bytes 1572872 | tf_op jit(solution)/shard_map/ppermute | solution.py:11
  9.5 14.0 %collective-permute-start.3 = (f32[1024,128]{1,0:T(8,128)}, f32[1024,128]{1,0:T(8,128)S(1)}, u32[]{:S(2)}, u32[]{:S(2)}) collective-permute-start(f32[1024,128]{1,0:T(8,128)} %param.3), channel_id=1, source_target_pairs={{0,16},{4,20},{8,24},{12,28},{16,0},{20,4},{24,8},{28,12},{1,17},{... | collective-permute-start | bytes 1572872 | tf_op jit(solution)/shard_map/ppermute | solution.py:11
  11.0 18.6 %collective-permute-start = (f32[1024,128]{1,0:T(8,128)}, f32[1024,128]{1,0:T(8,128)S(1)}, u32[]{:S(2)}, u32[]{:S(2)}) collective-permute-start(f32[1024,128]{1,0:T(8,128)} %param.3), channel_id=1, source_target_pairs={{0,4},{4,0},{8,12},{12,8},{16,20},{20,16},{24,28},{28,24},{1,5},{5... | collective-permute-start | bytes 1572872 | tf_op jit(solution)/shard_map/ppermute | solution.py:11
  47.5 157.0 %reduce-scatter.9.cloned.1.call-start = ((), (), s32[]{:S(2)}) async-start(), calls=%async_computation.8 | async-start | bytes 7864320 | tf_op jit(solution)/shard_map/reduce_scatter | solution.py:109
  69.5 248.7 %reduce-scatter.13.cloned.1.call-start = ((), (), s32[]{:S(2)}) async-start(), calls=%async_computation.10 | async-start | bytes 7864320 | tf_op jit(solution)/shard_map/reduce_scatter | solution.py:109
  91.5 306.2 %reduce-scatter.15.cloned.1.call-start = ((), (), s32[]{:S(2)}) async-start(), calls=%async_computation.11 | async-start | bytes 5242880 | tf_op jit(solution)/shard_map/reduce_scatter | solution.py:109
  98.1 18.7 %collective-permute-start.8 = (f32[512,256]{0,1:T(8,128)}, f32[512,256]{0,1:T(8,128)}, u32[]{:S(2)}, u32[]{:S(2)}) collective-permute-start(f32[512,256]{0,1:T(8,128)} %reduce-scatter.11.cloned.1.call-done), channel_id=1, source_target_pairs={{0,4},{4,0},{8,12},{12,8},{16,20},{20,16},{24,28},{28,24},{1,5},{5... | collective-permute-start | bytes 1572872 | tf_op jit(solution)/shard_map/ppermute | solution.py:11
  98.6 14.2 %collective-permute-start.9 = (f32[512,256]{0,1:T(8,128)}, f32[512,256]{0,1:T(8,128)}, u32[]{:S(2)}, u32[]{:S(2)}) collective-permute-start(f32[512,256]{0,1:T(8,128)} %reduce-scatter.11.cloned.1.call-done), channel_id=1, source_target_pairs={{0,8},{4,12},{8,0},{12,4},{16,24},{20,28},{24,16},{28,20},{1,9},{5... | collective-permute-start | bytes 1572872 | tf_op jit(solution)/shard_map/ppermute | solution.py:11
  100.1 15.1 %collective-permute-start.11 = (f32[512,256]{0,1:T(8,128)}, f32[512,256]{0,1:T(8,128)S(1)}, u32[]{:S(2)}, u32[]{:S(2)}) collective-permute-start(f32[512,256]{0,1:T(8,128)} %reduce-scatter.11.cloned.1.call-done), channel_id=1, source_target_pairs={{0,16},{4,20},{8,24},{12,28},{16,0},{20,4},{24,8},{28,12},{1,17},{... | collective-permute-start | bytes 1572872 | tf_op jit(solution)/shard_map/ppermute | solution.py:11
  113.8 13.4 %collective-permute-start.13 = (f32[256,256]{0,1:T(8,128)S(1)}, f32[256,256]{0,1:T(8,128)S(1)}, u32[]{:S(2)}, u32[]{:S(2)}) collective-permute-start(f32[256,256]{0,1:T(8,128)S(1)} %slice.335), channel_id=1, source_target_pairs={{0,16},{4,20},{8,24},{12,28},{16,0},{20,4},{24,8},{28,12},{1,17},{... | collective-permute-start | bytes 786440 | tf_op jit(solution)/shard_map/ppermute | solution.py:11
  116.3 13.3 %collective-permute-start.10 = (f32[512,256]{0,1:T(8,128)}, f32[512,256]{0,1:T(8,128)S(1)}, u32[]{:S(2)}, u32[]{:S(2)}) collective-permute-start(f32[512,256]{0,1:T(8,128)} %collective-permute-done.9), channel_id=1, source_target_pairs={{0,4},{4,0},{8,12},{12,8},{16,20},{20,16},{24,28},{28,24},{1,5},{5... | collective-permute-start | bytes 1572872 | tf_op jit(solution)/shard_map/ppermute | solution.py:11
  116.3 15.5 %collective-permute-start.12 = (f32[512,256]{0,1:T(8,128)S(1)}, f32[512,256]{0,1:T(8,128)S(1)}, u32[]{:S(2)}, u32[]{:S(2)}) collective-permute-start(f32[512,256]{0,1:T(8,128)S(1)} %collective-permute-done.11), channel_id=1, source_target_pairs={{0,4},{4,0},{8,12},{12,8},{16,20},{20,16},{24,28},{28,24},{1,5},{5... | collective-permute-start | bytes 1572872 | tf_op jit(solution)/shard_map/ppermute | solution.py:11
  204.5 246.8 %reduce-scatter.17.cloned.1.call-start = ((), (), s32[]{:S(2)}) async-start(), calls=%async_computation.12 | async-start | bytes 2621440 | tf_op jit(solution)/shard_map/reduce_scatter | solution.py:109
  206.1 36.2 %collective-permute-start.17 = (f32[512,768]{1,0:T(8,128)S(1)}, f32[512,768]{1,0:T(8,128)S(1)}, u32[]{:S(2)}, u32[]{:S(2)}) collective-permute-start(f32[512,768]{1,0:T(8,128)S(1)} %pad_maximum_fusion.3), channel_id=1, source_target_pairs={{0,8},{4,12},{8,0},{12,4},{16,24},{20,28},{24,16},{28,20},{1,9},{5... | collective-permute-start | bytes 4718600 | tf_op jit(solution)/shard_map/ppermute | solution.py:11
  207.6 36.3 %collective-permute-start.19 = (f32[512,768]{1,0:T(8,128)S(1)}, f32[512,768]{1,0:T(8,128)S(1)}, u32[]{:S(2)}, u32[]{:S(2)}) collective-permute-start(f32[512,768]{1,0:T(8,128)S(1)} %pad_maximum_fusion.3), channel_id=1, source_target_pairs={{0,16},{4,20},{8,24},{12,28},{16,0},{20,4},{24,8},{28,12},{1,17},{... | collective-permute-start | bytes 4718600 | tf_op jit(solution)/shard_map/ppermute | solution.py:11
  209.1 36.5 %collective-permute-start.16 = (f32[512,768]{1,0:T(8,128)S(1)}, f32[512,768]{1,0:T(8,128)S(1)}, u32[]{:S(2)}, u32[]{:S(2)}) collective-permute-start(f32[512,768]{1,0:T(8,128)S(1)} %pad_maximum_fusion.3), channel_id=1, source_target_pairs={{0,4},{4,0},{8,12},{12,8},{16,20},{20,16},{24,28},{28,24},{1,5},{5... | collective-permute-start | bytes 4718600 | tf_op jit(solution)/shard_map/ppermute | solution.py:11
  242.4 18.6 %collective-permute-start.21 = (f32[256,768]{1,0:T(8,128)S(1)}, f32[256,768]{1,0:T(8,128)S(1)}, u32[]{:S(2)}, u32[]{:S(2)}) collective-permute-start(f32[256,768]{1,0:T(8,128)S(1)} %slice.339), channel_id=1, source_target_pairs={{0,16},{4,20},{8,24},{12,28},{16,0},{20,4},{24,8},{28,12},{1,17},{... | collective-permute-start | bytes 2359304 | tf_op jit(solution)/shard_map/ppermute | solution.py:11
  244.0 18.4 %collective-permute-start.22 = (f32[256,768]{1,0:T(8,128)S(1)}, f32[256,768]{1,0:T(8,128)S(1)}, u32[]{:S(2)}, u32[]{:S(2)}) collective-permute-start(f32[256,768]{1,0:T(8,128)S(1)} %slice.340), channel_id=1, source_target_pairs={{0,8},{4,12},{8,0},{12,4},{16,24},{20,28},{24,16},{28,20},{1,9},{5... | collective-permute-start | bytes 2359304 | tf_op jit(solution)/shard_map/ppermute | solution.py:11
  248.1 18.2 %collective-permute-start.18 = (f32[512,768]{1,0:T(8,128)S(1)}, f32[512,768]{1,0:T(8,128)S(1)}, u32[]{:S(2)}, u32[]{:S(2)}) collective-permute-start(f32[512,768]{1,0:T(8,128)S(1)} %collective-permute-done.17), channel_id=1, source_target_pairs={{0,4},{4,0},{8,12},{12,8},{16,20},{20,16},{24,28},{28,24},{1,5},{5... | collective-permute-start | bytes 4718600 | tf_op jit(solution)/shard_map/ppermute | solution.py:11
  249.4 19.5 %collective-permute-start.20 = (f32[512,768]{1,0:T(8,128)S(1)}, f32[512,768]{1,0:T(8,128)S(1)}, u32[]{:S(2)}, u32[]{:S(2)}) collective-permute-start(f32[512,768]{1,0:T(8,128)S(1)} %collective-permute-done.19), channel_id=1, source_target_pairs={{0,4},{4,0},{8,12},{12,8},{16,20},{20,16},{24,28},{28,24},{1,5},{5... | collective-permute-start | bytes 4718600 | tf_op jit(solution)/shard_map/ppermute | solution.py:11
  319.8 36.4 %collective-permute-start.25 = (f32[512,768]{1,0:T(8,128)S(1)}, f32[512,768]{1,0:T(8,128)}, u32[]{:S(2)}, u32[]{:S(2)}) collective-permute-start(f32[512,768]{1,0:T(8,128)S(1)} %pad_maximum_fusion.4), channel_id=1, source_target_pairs={{0,8},{4,12},{8,0},{12,4},{16,24},{20,28},{24,16},{28,20},{1,9},{5... | collective-permute-start | bytes 4718600 | tf_op jit(solution)/shard_map/ppermute | solution.py:11
  321.3 37.6 %collective-permute-start.27 = (f32[512,768]{1,0:T(8,128)S(1)}, f32[512,768]{1,0:T(8,128)}, u32[]{:S(2)}, u32[]{:S(2)}) collective-permute-start(f32[512,768]{1,0:T(8,128)S(1)} %pad_maximum_fusion.4), channel_id=1, source_target_pairs={{0,16},{4,20},{8,24},{12,28},{16,0},{20,4},{24,8},{28,12},{1,17},{... | collective-permute-start | bytes 4718600 | tf_op jit(solution)/shard_map/ppermute | solution.py:11
  322.8 38.8 %collective-permute-start.24 = (f32[512,768]{1,0:T(8,128)S(1)}, f32[512,768]{1,0:T(8,128)}, u32[]{:S(2)}, u32[]{:S(2)}) collective-permute-start(f32[512,768]{1,0:T(8,128)S(1)} %pad_maximum_fusion.4), channel_id=1, source_target_pairs={{0,4},{4,0},{8,12},{12,8},{16,20},{20,16},{24,28},{28,24},{1,5},{5... | collective-permute-start | bytes 4718600 | tf_op jit(solution)/shard_map/ppermute | solution.py:11
  334.1 155.7 %reduce-scatter.19.cloned.1.call-start = ((), (), s32[]{:S(2)}) async-start(), calls=%async_computation.13 | async-start | bytes 2621440 | tf_op jit(solution)/shard_map/reduce_scatter | solution.py:109
  357.3 18.6 %collective-permute-start.29 = (f32[256,768]{1,0:T(8,128)S(1)}, f32[256,768]{1,0:T(8,128)S(1)}, u32[]{:S(2)}, u32[]{:S(2)}) collective-permute-start(f32[256,768]{1,0:T(8,128)S(1)} %slice.343), channel_id=1, source_target_pairs={{0,16},{4,20},{8,24},{12,28},{16,0},{20,4},{24,8},{28,12},{1,17},{... | collective-permute-start | bytes 2359304 | tf_op jit(solution)/shard_map/ppermute | solution.py:11
  360.1 18.3 %collective-permute-start.30 = (f32[256,768]{1,0:T(8,128)S(1)}, f32[256,768]{1,0:T(8,128)S(1)}, u32[]{:S(2)}, u32[]{:S(2)}) collective-permute-start(f32[256,768]{1,0:T(8,128)S(1)} %slice.344), channel_id=1, source_target_pairs={{0,8},{4,12},{8,0},{12,4},{16,24},{20,28},{24,16},{28,20},{1,9},{5... | collective-permute-start | bytes 2359304 | tf_op jit(solution)/shard_map/ppermute | solution.py:11
  366.4 17.0 %collective-permute-start.26 = (f32[512,768]{1,0:T(8,128)}, f32[512,768]{1,0:T(8,128)S(1)}, u32[]{:S(2)}, u32[]{:S(2)}) collective-permute-start(f32[512,768]{1,0:T(8,128)} %collective-permute-done.25), channel_id=1, source_target_pairs={{0,4},{4,0},{8,12},{12,8},{16,20},{20,16},{24,28},{28,24},{1,5},{5... | collective-permute-start | bytes 4718600 | tf_op jit(solution)/shard_map/ppermute | solution.py:11
  368.8 17.2 %collective-permute-start.28 = (f32[512,768]{1,0:T(8,128)}, f32[512,768]{1,0:T(8,128)S(1)}, u32[]{:S(2)}, u32[]{:S(2)}) collective-permute-start(f32[512,768]{1,0:T(8,128)} %collective-permute-done.27), channel_id=1, source_target_pairs={{0,4},{4,0},{8,12},{12,8},{16,20},{20,16},{24,28},{28,24},{1,5},{5... | collective-permute-start | bytes 4718600 | tf_op jit(solution)/shard_map/ppermute | solution.py:11
  400.1 25.3 %collective-permute-start.33 = (f32[512,512]{1,0:T(8,128)}, f32[512,512]{1,0:T(8,128)}, u32[]{:S(2)}, u32[]{:S(2)}) collective-permute-start(f32[512,512]{1,0:T(8,128)} %pad_maximum_fusion.5), channel_id=1, source_target_pairs={{0,8},{4,12},{8,0},{12,4},{16,24},{20,28},{24,16},{28,20},{1,9},{5... | collective-permute-start | bytes 3145736 | tf_op jit(solution)/shard_map/ppermute | solution.py:11
  401.6 26.4 %collective-permute-start.35 = (f32[512,512]{1,0:T(8,128)}, f32[512,512]{1,0:T(8,128)}, u32[]{:S(2)}, u32[]{:S(2)}) collective-permute-start(f32[512,512]{1,0:T(8,128)} %pad_maximum_fusion.5), channel_id=1, source_target_pairs={{0,16},{4,20},{8,24},{12,28},{16,0},{20,4},{24,8},{28,12},{1,17},{... | collective-permute-start | bytes 3145736 | tf_op jit(solution)/shard_map/ppermute | solution.py:11
  403.1 29.7 %collective-permute-start.32 = (f32[512,512]{1,0:T(8,128)}, f32[512,512]{1,0:T(8,128)}, u32[]{:S(2)}, u32[]{:S(2)}) collective-permute-start(f32[512,512]{1,0:T(8,128)} %pad_maximum_fusion.5), channel_id=1, source_target_pairs={{0,4},{4,0},{8,12},{12,8},{16,20},{20,16},{24,28},{28,24},{1,5},{5... | collective-permute-start | bytes 3145736 | tf_op jit(solution)/shard_map/ppermute | solution.py:11
  414.2 121.1 %reduce-scatter.21.cloned.1.call-start = ((), (), s32[]{:S(2)}) async-start(), calls=%async_computation.14 | async-start | bytes 2621440 | tf_op jit(solution)/shard_map/reduce_scatter | solution.py:109
  426.5 17.6 %collective-permute-start.37 = (f32[256,512]{1,0:T(8,128)S(1)}, f32[256,512]{1,0:T(8,128)S(1)}, u32[]{:S(2)}, u32[]{:S(2)}) collective-permute-start(f32[256,512]{1,0:T(8,128)S(1)} %slice.349), channel_id=1, source_target_pairs={{0,16},{4,20},{8,24},{12,28},{16,0},{20,4},{24,8},{28,12},{1,17},{... | collective-permute-start | bytes 1572872 | tf_op jit(solution)/shard_map/ppermute | solution.py:11
  429.1 15.1 %collective-permute-start.38 = (f32[256,512]{1,0:T(8,128)S(1)}, f32[256,512]{1,0:T(8,128)S(1)}, u32[]{:S(2)}, u32[]{:S(2)}) collective-permute-start(f32[256,512]{1,0:T(8,128)S(1)} %slice.350), channel_id=1, source_target_pairs={{0,8},{4,12},{8,0},{12,4},{16,24},{20,28},{24,16},{28,20},{1,9},{5... | collective-permute-start | bytes 1572872 | tf_op jit(solution)/shard_map/ppermute | solution.py:11
  451.3 18.7 %collective-permute-start.40 = (f32[512,256]{0,1:T(8,128)}, f32[512,256]{0,1:T(8,128)}, u32[]{:S(2)}, u32[]{:S(2)}) collective-permute-start(f32[512,256]{0,1:T(8,128)} %reduce-scatter.17.cloned.1.call-done), channel_id=1, source_target_pairs={{0,4},{4,0},{8,12},{12,8},{16,20},{20,16},{24,28},{28,24},{1,5},{5... | collective-permute-start | bytes 1572872 | tf_op jit(solution)/shard_map/ppermute | solution.py:11
  451.9 15.1 %collective-permute-start.41 = (f32[512,256]{0,1:T(8,128)}, f32[512,256]{0,1:T(8,128)S(1)}, u32[]{:S(2)}, u32[]{:S(2)}) collective-permute-start(f32[512,256]{0,1:T(8,128)} %reduce-scatter.17.cloned.1.call-done), channel_id=1, source_target_pairs={{0,8},{4,12},{8,0},{12,4},{16,24},{20,28},{24,16},{28,20},{1,9},{5... | collective-permute-start | bytes 1572872 | tf_op jit(solution)/shard_map/ppermute | solution.py:11
  452.4 16.0 %collective-permute-start.43 = (f32[512,256]{0,1:T(8,128)}, f32[512,256]{0,1:T(8,128)S(1)}, u32[]{:S(2)}, u32[]{:S(2)}) collective-permute-start(f32[512,256]{0,1:T(8,128)} %reduce-scatter.17.cloned.1.call-done), channel_id=1, source_target_pairs={{0,16},{4,20},{8,24},{12,28},{16,0},{20,4},{24,8},{28,12},{1,17},{... | collective-permute-start | bytes 1572872 | tf_op jit(solution)/shard_map/ppermute | solution.py:11
  464.3 187.0 %reduce-scatter.23.cloned.1.call-start = ((), (), s32[]{:S(2)}) async-start(), calls=%async_computation.15 | async-start | bytes 5898240 | tf_op jit(solution)/shard_map/reduce_scatter | solution.py:125
  466.9 12.1 %collective-permute-start.45 = (f32[256,256]{0,1:T(8,128)S(1)}, f32[256,256]{0,1:T(8,128)S(1)}, u32[]{:S(2)}, u32[]{:S(2)}) collective-permute-start(f32[256,256]{0,1:T(8,128)S(1)} %slice.351), channel_id=1, source_target_pairs={{0,16},{4,20},{8,24},{12,28},{16,0},{20,4},{24,8},{28,12},{1,17},{... | collective-permute-start | bytes 786440 | tf_op jit(solution)/shard_map/ppermute | solution.py:11
  489.8 13.7 %collective-permute-start.49 = (f32[512,256]{0,1:T(8,128)}, f32[512,256]{0,1:T(8,128)S(1)}, u32[]{:S(2)}, u32[]{:S(2)}) collective-permute-start(f32[512,256]{0,1:T(8,128)} %reduce-scatter.19.cloned.1.call-done), channel_id=1, source_target_pairs={{0,8},{4,12},{8,0},{12,4},{16,24},{20,28},{24,16},{28,20},{1,9},{5... | collective-permute-start | bytes 1572872 | tf_op jit(solution)/shard_map/ppermute | solution.py:11
  491.2 13.8 %collective-permute-start.51 = (f32[512,256]{0,1:T(8,128)}, f32[512,256]{0,1:T(8,128)S(1)}, u32[]{:S(2)}, u32[]{:S(2)}) collective-permute-start(f32[512,256]{0,1:T(8,128)} %reduce-scatter.19.cloned.1.call-done), channel_id=1, source_target_pairs={{0,16},{4,20},{8,24},{12,28},{16,0},{20,4},{24,8},{28,12},{1,17},{... | collective-permute-start | bytes 1572872 | tf_op jit(solution)/shard_map/ppermute | solution.py:11
  492.7 13.9 %collective-permute-start.48 = (f32[512,256]{0,1:T(8,128)}, f32[512,256]{0,1:T(8,128)S(1)}, u32[]{:S(2)}, u32[]{:S(2)}) collective-permute-start(f32[512,256]{0,1:T(8,128)} %reduce-scatter.19.cloned.1.call-done), channel_id=1, source_target_pairs={{0,4},{4,0},{8,12},{12,8},{16,20},{20,16},{24,28},{28,24},{1,5},{5... | collective-permute-start | bytes 1572872 | tf_op jit(solution)/shard_map/ppermute | solution.py:11
  535.3 13.8 %collective-permute-start.57 = (f32[512,256]{0,1:T(8,128)}, f32[512,256]{0,1:T(8,128)S(1)}, u32[]{:S(2)}, u32[]{:S(2)}) collective-permute-start(f32[512,256]{0,1:T(8,128)} %reduce-scatter.21.cloned.1.call-done), channel_id=1, source_target_pairs={{0,8},{4,12},{8,0},{12,4},{16,24},{20,28},{24,16},{28,20},{1,9},{5... | collective-permute-start | bytes 1572872 | tf_op jit(solution)/shard_map/ppermute | solution.py:11
  536.8 13.8 %collective-permute-start.59 = (f32[512,256]{0,1:T(8,128)}, f32[512,256]{0,1:T(8,128)S(1)}, u32[]{:S(2)}, u32[]{:S(2)}) collective-permute-start(f32[512,256]{0,1:T(8,128)} %reduce-scatter.21.cloned.1.call-done), channel_id=1, source_target_pairs={{0,16},{4,20},{8,24},{12,28},{16,0},{20,4},{24,8},{28,12},{1,17},{... | collective-permute-start | bytes 1572872 | tf_op jit(solution)/shard_map/ppermute | solution.py:11
  538.3 14.4 %collective-permute-start.56 = (f32[512,256]{0,1:T(8,128)}, f32[512,256]{0,1:T(8,128)S(1)}, u32[]{:S(2)}, u32[]{:S(2)}) collective-permute-start(f32[512,256]{0,1:T(8,128)} %reduce-scatter.21.cloned.1.call-done), channel_id=1, source_target_pairs={{0,4},{4,0},{8,12},{12,8},{16,20},{20,16},{24,28},{28,24},{1,5},{5... | collective-permute-start | bytes 1572872 | tf_op jit(solution)/shard_map/ppermute | solution.py:11
  665.2 15.4 %collective-permute-start.75 = (f32[128,128]{1,0:T(8,128)S(1)}, f32[128,128]{1,0:T(8,128)S(1)}, u32[]{:S(2)}, u32[]{:S(2)}) collective-permute-start(f32[128,128]{1,0:T(8,128)S(1)} %bitcast.140), channel_id=1, source_target_pairs={{0,8},{1,9},{2,10},{3,11},{4,12},{5,13},{6,14},{7,15},{8,2},{9,3},... | collective-permute-start | bytes 196616 | tf_op jit(solution)/shard_map/ppermute | solution.py:83
  669.7 12.2 %collective-permute-start.68 = (f32[128,128]{1,0:T(8,128)S(1)}, f32[128,128]{1,0:T(8,128)S(1)}, u32[]{:S(2)}, u32[]{:S(2)}) collective-permute-start(f32[128,128]{1,0:T(8,128)S(1)} %bitcast.139), channel_id=1, source_target_pairs={{0,21},{1,20},{2,23},{3,22},{4,17},{5,16},{6,19},{7,18},{8,29},{9,... | collective-permute-start | bytes 196616 | tf_op jit(solution)/shard_map/ppermute | solution.py:83
  (131 other events, 717.7 us)
Sparse Core Ops, SparseCore 0:
  47.6 44.2 reduce-scatter.10
  94.3 110.0 reduce-scatter.8
  206.9 111.2 reduce-scatter.12
  320.4 77.2 reduce-scatter.14
  399.9 44.3 reduce-scatter.16
  446.5 43.1 reduce-scatter.18
  492.1 43.1 reduce-scatter.20
  567.6 83.6 reduce-scatter.22
